TPU v7x, 32 devices: a whole 2x2x4 slice. The times are simulated.
32 devices in a mesh: depth: 8 (over z, y), tile: 4 (over x, core).
Axes of the slice: x: 2, y: 2, z: 4, core: 2. Of those that a mesh axis runs over, the one named last changes fastest.
Arguments:
- volume: bfloat16 [96, 4, 768, 512], P('depth', 'tile'), may hold values from -6 to 6
- table_index: int32 [96, 4, 768, 32], P('depth', 'tile'), may hold values from 0 to 15
- brick_position: int32 [8], replicated, may hold values from 0 to 7, each once
- tf_center: float32 [16], replicated, may hold values from -1.5 to 1.5
- tf_width: float32 [16], replicated, may hold values from 0.3 to 1.2
- tf_peak: float32 [16], replicated, may hold values from 2 to 32
- tf_color: float32 [3, 16], replicated, may hold values from 0.1 to 1
Outputs:
- frame: float32 [4, 4, 768, 512], P(None, 'tile', 'depth')
Inputs may be any that keep to these rules, and one draw needn't show every extreme that they name: `brick_position`: each depth rank has a different position.
All inputs are finite; a program needn't handle non-finite values.
Results may differ from a plain program's by a relative error of at most 0.0003.
Values may be sent and summed in bfloat16 or wider, within the bound.
A program may use at most 128 MiB of HBM per device.

v0:
```python
import jax
import jax.numpy as jnp
from jax import lax
from jax.sharding import PartitionSpec as P

CELL = 16


def from_partner(value, axis, apart):
    return lax.ppermute(value, axis, [(i, i ^ 1 << apart) for i in range(lax.axis_size(axis))])


def light_sample(value, grad_x, grad_y, params, rgb, trans, inverse):
    energy = grad_x * grad_x + grad_y * grad_y
    facing = 0.6 * grad_x + 0.8 * grad_y
    shade = 0.3 + 0.7 * facing * facing / (1.0 + energy)
    scaled = (value - params[0]) / params[1]
    extinction = params[2] * jnp.exp(-0.5 * scaled * scaled) * energy * inverse
    keep = jnp.exp(-extinction)
    opacity = 1.0 - keep
    weight = trans * opacity
    rgb = rgb + weight[None] * params[3:6] * shade[None]
    trans = trans * keep
    return (rgb, trans)


def composite(layers):
    while layers.shape[1] > 1:
        front = layers[:, 0::2]
        back = layers[:, 1::2]
        layers = front + (1.0 - front[3:4]) * back
    return layers[:, 0]


def on_device(volume, table_index, brick_position, tf_center, tf_width, tf_peak, tf_color):
    tables = jnp.concatenate([tf_center[None], tf_width[None], tf_peak[None], tf_color], axis=0)
    samples = volume[:, 0]
    cells = table_index[:, 0]
    depth_count = samples.shape[0]
    height = samples.shape[1]
    width = samples.shape[2]
    cell_count = cells.shape[2]
    table_count = tables.shape[1]
    param_count = tables.shape[0]
    ranks = lax.axis_size("depth")
    inverse = 1.0 / (depth_count * ranks)
    tile_rank = lax.axis_index("tile")
    col_bit = tile_rank % 2
    row_bit = tile_rank // 2
    send_col = jnp.where(col_bit == 0, samples[:, :, width - 1], samples[:, :, 0])
    got_col = from_partner(send_col, "tile", 0)
    send_row = jnp.where(row_bit == 0, samples[:, height - 1, :], samples[:, 0, :])
    got_row = from_partner(send_row, "tile", 1)
    zero_col = jnp.zeros_like(got_col)
    zero_row = jnp.zeros_like(got_row)
    left_rim = jnp.where(col_bit == 1, got_col, zero_col)
    right_rim = jnp.where(col_bit == 0, got_col, zero_col)
    top_rim = jnp.where(row_bit == 1, got_row, zero_row)
    bottom_rim = jnp.where(row_bit == 0, got_row, zero_row)
    wide_pad = jnp.concatenate([left_rim[:, :, None], samples, right_rim[:, :, None]], axis=2)
    tall_pad = jnp.concatenate([top_rim[:, None, :], samples, bottom_rim[:, None, :]], axis=1)
    entries = jnp.arange(table_count, dtype=jnp.int32)
    table_grid = tables[:, :, None, None]

    def sample(step, carry):
        rgb, trans = carry
        wide = lax.dynamic_index_in_dim(wide_pad, step, 0, keepdims=False).astype(jnp.float32)
        tall = lax.dynamic_index_in_dim(tall_pad, step, 0, keepdims=False).astype(jnp.float32)
        cell_index = lax.dynamic_index_in_dim(cells, step, 0, keepdims=False)
        matches_cell = cell_index[None] == entries[:, None, None]
        cell_params = jnp.sum(jnp.where(matches_cell[None], table_grid, 0.0), axis=1)
        params = jnp.broadcast_to(cell_params[..., None], (param_count, height, cell_count, CELL))
        params = params.reshape(param_count, height, width)
        value = wide[:, 1:-1]
        grad_x = 0.5 * (wide[:, 2:] - wide[:, :-2])
        grad_y = 0.5 * (tall[2:, :] - tall[:-2, :])
        return light_sample(value, grad_x, grad_y, params, rgb, trans, inverse)

    start = (jnp.zeros((3, height, width), jnp.float32), jnp.ones((height, width), jnp.float32))
    rgb, trans = lax.fori_loop(0, depth_count, sample, start)
    partial_value = jnp.concatenate([rgb, (1.0 - trans)[None]], axis=0)
    piece_rows = height // ranks
    places = jnp.arange(ranks, dtype=jnp.int32)
    matches = brick_position[None, :] == places[:, None]
    rank_at = jnp.sum(jnp.where(matches, places[None, :], 0), axis=1)
    received = lax.all_to_all(partial_value, "depth", split_axis=1, concat_axis=0, tiled=True)
    stacked = received.reshape(ranks, 4, piece_rows, received.shape[2])
    ordered = jnp.take(stacked, rank_at, axis=0)
    image = composite(jnp.moveaxis(ordered, 0, 1))
    return image[:, None]


def solution(mesh):
    return jax.shard_map(
        on_device,
        mesh=mesh,
        in_specs=(
            P("depth", "tile", None, None),
            P("depth", "tile", None, None),
            P(),
            P(),
            P(),
            P(),
            P(),
        ),
        out_specs=P(None, "tile", "depth", None),
        check_vma=False,
    )
```

profile of v0, /device:TPU:0, one launch (start us, length us, event | category | flops | bytes accessed | tf_op | source)
XLA Modules:
  0.0 373.2 jit_solution(8455016946982485030)
XLA Ops:
  0.0 16.3 %copy.60 = bf16[12,1,768,512]{2,0,3,1:T(8,128)(2,1)} copy(bf16[12,1,768,512]{3,2,1,0:T(8,128)(2,1)} %param.9) | data formatting | bytes 18874368 | tf_op args[0]
  16.3 2.9 slice_select_fusion
  20.9 3.0 collective-permute-start.1
  25.6 2.9 copy.62
  28.5 2.9 copy.63
  31.4 12.8 %pad_maximum_fusion = bf16[12,770,512]{1,0,2:T(8,128)(2,1)S(1)} fusion(bf16[12,1,512]{1,0,2:T(8,128)(2,1)} %copy.63, bf16[12,768,512]{1,0,2:T(8,128)(2,1)} %bitcast.88, bf16[12,1,512]{1,0,2:T(8,128)(2,1)} %copy.62), kind=kLoop, calls=%fused_computation.31 | loop fusion | flops 28385280 | bytes 18923520 | tf_op jit(solution)/shard_map/concatenate | solution.py:61
  44.2 5.4 %copy.65 = bf16[12,770,512]{1,2,0:T(8,128)(2,1)} copy(bf16[12,770,512]{1,0,2:T(8,128)(2,1)S(1)} %pad_maximum_fusion) | data formatting | bytes 18923520
  49.7 3.0 pad_maximum_fusion.1
  52.7 5.6 %copy.64 = bf16[12,768,514]{1,2,0:T(8,128)(2,1)} copy(bf16[12,768,514]{1,0,2:T(8,128)(2,1)S(1)} %pad_maximum_fusion.1) | data formatting | bytes 18948096
  58.3 133.2 %while.18 = (s32[]{:T(128)}, f32[3,768,512]{1,2,0:T(8,128)}, f32[768,512]{0,1:T(8,128)S(1)}, s32[12,768,32]{1,2,0:T(8,128)}, f32[6,16,1,1]{1,0,3,2:T(8,128)S(1)}...) while((s32[]{:T(128)}, f32[3,768,512]{1,2,0:T(8,128)}, ...), condition=%wide.region_3.4_spmd.clone, body=%wide.region_1.3_spmd.clone.sunk | while | flops 21481988 | bytes 75808312 | solution.py:80
  67.1 2.2 copy-done
  78.2 2.2 copy-done
  89.3 2.2 copy-done
  100.4 2.2 copy-done
  122.6 2.2 copy-done
  133.7 2.2 copy-done
  144.8 2.2 copy-done
  191.5 7.3 %copy.67 = f32[3,768,512]{2,0,1:T(4,128)} copy(f32[3,768,512]{1,2,0:T(8,128)} %get-tuple-element.205) | data formatting | bytes 9437184 | tf_op jit(solution)/shard_map/while | solution.py:80
  200.5 8.3 %pad_maximum_fusion.2 = f32[4,768,512]{2,0,1:T(4,128)} fusion(f32[1,768,512]{2,0,1:T(1,128)S(1)} %broadcast_in_dim.173, f32[3,768,512]{2,0,1:T(4,128)} %copy.67), kind=kLoop, calls=%fused_computation.33 | loop fusion | flops 1572864 | bytes 12582912 | tf_op jit(solution)/shard_map/concatenate | solution.py:81
  208.7 6.5 %all-to-all-start = ((f32[4,768,512]{2,0,1:T(4,128)}), f32[4,768,512]{2,0,1:T(4,128)}, u32[]{:S(2)}, u32[]{:S(2)}) async-start(f32[4,768,512]{2,0,1:T(4,128)} %pad_maximum_fusion.2), calls=%async_computation | async-start | bytes 12582912 | tf_op jit(solution)/shard_map/all_to_all | solution.py:86
  215.4 137.3 %all-to-all-done = f32[4,768,512]{2,0,1:T(4,128)} async-done(((f32[4,768,512]{2,0,1:T(4,128)}), f32[4,768,512]{2,0,1:T(4,128)}, u32[]{:S(2)}, u32[]{:S(2)}) %all-to-all-start) | async-done | bytes 6291488 | tf_op jit(solution)/shard_map/all_to_all | solution.py:86
  352.7 7.3 %copy.74 = f32[4,8,96,512]{3,2,0,1:T(8,128)} copy(f32[4,8,96,512]{3,0,2,1:T(4,128)} %bitcast.12) | data formatting | bytes 12582912 | tf_op jit(solution)/shard_map/all_to_all | solution.py:86
  360.0 6.4 %gather_fusion = f32[8,4,96,512]{3,2,1,0:T(8,128)} fusion(f32[8,4,96,512]{3,2,1,0:T(8,128)} %bitcast.92, s32[1024]{0:T(1024)S(1)} %pad_clamp_fusion), kind=kCustom, calls=%fused_computation | custom fusion | bytes 12582944 | tf_op jit(solution)/shard_map/jit(_take)/gather | solution.py:88
  366.4 3.6 select_bitcast_fusion
  (251 shorter events, 124.8 us)
Async XLA Ops:
  19.2 5.5 %copy-start.1 = (f32[3,16]{1,0:T(4,128)S(1)}, f32[3,16]{1,0:T(4,128)}, u32[]{:S(2)}) copy-start(f32[3,16]{1,0:T(4,128)} %param.15) | copy-start | bytes 580
  19.2 5.5 %copy-start.2 = (f32[16]{0:T(128)S(1)}, f32[16]{0:T(128)}, u32[]{:S(2)}) copy-start(f32[16]{0:T(128)} %param.14) | copy-start | bytes 196
  19.2 5.5 %copy-start.3 = (f32[16]{0:T(128)S(1)}, f32[16]{0:T(128)}, u32[]{:S(2)}) copy-start(f32[16]{0:T(128)} %param.13) | copy-start | bytes 196
  19.2 5.5 %copy-start.4 = (f32[16]{0:T(128)S(1)}, f32[16]{0:T(128)}, u32[]{:S(2)}) copy-start(f32[16]{0:T(128)} %param.12) | copy-start | bytes 196
  20.9 4.7 %collective-permute-start.1 = (bf16[12,512]{1,0:T(8,128)(2,1)S(1)}, bf16[12,512]{1,0:T(8,128)(2,1)S(1)}, u32[]{:S(2)}, u32[]{:S(2)}) collective-permute-start(bf16[12,512]{1,0:T(8,128)(2,1)S(1)} %bitcast.95), channel_id=1, source_target_pairs={{0,2},{1,3},{2,0},{3,1},{4,6},{5,7},{6,4},{7,5},{8,10},{9,11},{10,... | collective-permute-start | bytes 36872 | tf_op jit(solution)/shard_map/ppermute | solution.py:10
  24.7 25.0 %collective-permute-start = (bf16[12,768]{1,0:T(8,128)(2,1)S(1)}, bf16[12,768]{1,0:T(8,128)(2,1)S(1)}, u32[]{:S(2)}, u32[]{:S(2)}) collective-permute-start(bf16[12,768]{1,0:T(8,128)(2,1)S(1)} %fusion.18), channel_id=1, source_target_pairs={{0,1},{1,0},{2,3},{3,2},{4,5},{5,4},{6,7},{7,6},{8,9},{9,8},{10,11... | collective-permute-start | bytes 55304 | tf_op jit(solution)/shard_map/ppermute | solution.py:10
  31.4 18.3 %slice-start.2 = ((s8[12582912]{0:T(1024)(128)(4,1)}), s8[4194304]{0:T(1024)(128)(4,1)S(1)}, s32[]{:S(2)}) async-start(s8[12582912]{0:T(1024)(128)(4,1)} %bitcast.89), calls=%async_computation.3 | async-start | bytes 8388608
  31.4 18.3 %slice-start.3 = ((s8[12582912]{0:T(1024)(128)(4,1)}), s8[4194304]{0:T(1024)(128)(4,1)S(1)}, s32[]{:S(2)}) async-start(s8[12582912]{0:T(1024)(128)(4,1)} %bitcast.89), calls=%async_computation.4 | async-start | bytes 8388608
  44.2 5.4 %slice-start.4 = ((s8[12582912]{0:T(1024)(128)(4,1)}), s8[4194304]{0:T(1024)(128)(4,1)S(1)}, s32[]{:S(2)}) async-start(s8[12582912]{0:T(1024)(128)(4,1)} %bitcast.89), calls=%async_computation.5 | async-start | bytes 8388608
  62.9 2.3 slice-start.1
  74.0 2.2 slice-start
  74.0 2.3 slice-start.1
  85.1 2.3 slice-start.1
  96.2 2.3 slice-start.1
  107.3 2.3 slice-start.1
  118.4 2.3 slice-start.1
  129.5 2.3 slice-start.1
  140.6 2.3 slice-start.1
  151.7 2.3 slice-start.1
  162.8 2.3 slice-start.1
  173.9 2.3 slice-start.1
  185.0 2.3 slice-start.1
  208.7 6.5 %copy-start.5 = (s32[8]{0:T(128)S(1)}, s32[8]{0:T(128)}, u32[]{:S(2)}) copy-start(s32[8]{0:T(128)} %param.11) | copy-start | bytes 100
  208.7 144.0 %all-to-all-start = ((f32[4,768,512]{2,0,1:T(4,128)}), f32[4,768,512]{2,0,1:T(4,128)}, u32[]{:S(2)}, u32[]{:S(2)}) async-start(f32[4,768,512]{2,0,1:T(4,128)} %pad_maximum_fusion.2), calls=%async_computation | async-start | bytes 12582912 | tf_op jit(solution)/shard_map/all_to_all | solution.py:86
  (23 other events, 51.3 us)
where the time goes:
time: 376 us; the launch traced here: 373 us
  waiting for transfers between devices  138 us (37%)
  other arithmetic  126 us (34%)
  local copies, waits for them, and re-layouts  97.7 us (26%)
  starting transfers between devices  9.5 us (3%)
    all_to_all x1, waiting for transfers between devices, on_device(): lax.all_to_all(partial_value, 'depth', split_axis=1, concat_axis=0, tiled...  137 us
    while x84, local copies, waits for them, and re-layouts  28.5 us
    unnamed x19, local copies, waits for them, and re-layouts  27.4 us
    mul x12, other arithmetic, light_sample(): trans = trans * keep  22.4 us
    add x12, other arithmetic, light_sample(): rgb = rgb + weight[None] * params[3:6] * shade[None]  21.8 us
    convert_element_type x12, other arithmetic, sample(): lax.dynamic_index_in_dim(tall_pad, step, 0, keepdims=False)  15.7 us
    convert_element_type x12, other arithmetic, sample(): lax.dynamic_index_in_dim(wide_pad, step, 0, keepdims=False)  15 us
    concatenate x1, other arithmetic, on_device(): jnp.concatenate([top_rim[:, None, :], samples, bottom_rim[:, None, :]], a...  12.8 us
  transfers between devices with their start and end apart: 3, of which 2 were waited for; matrix products, arithmetic and copies ran while one was open for 7% of the time, Pallas kernels for 0%

commit v1 on v0

--- a/solution.py
+++ b/solution.py
@@ -1,9 +1,358 @@
+import functools
+import math
 import jax
 import jax.numpy as jnp
 from jax import lax
+from jax.experimental import pallas as pl
+from jax.experimental.pallas import tpu as pltpu
 from jax.sharding import PartitionSpec as P
 
 CELL = 16
+ROWS = 16
+LANES = 128
+OCTAVES = 30.0
+TOP_CODE = 65535.0
+MID_CODE = 32768
+SCALE = TOP_CODE / OCTAVES
+LOG2E = 1.0 / math.log(2.0)
+PARTS = 3
+MESH = pl.DeviceIdType.MESH
+
+
+def encode(value):
+    code = jnp.log(value) * (-SCALE * LOG2E)
+    code = jnp.minimum(jnp.maximum(code, 0.0), TOP_CODE)
+    return ((code + 0.5).astype(jnp.int32) - MID_CODE).astype(jnp.int16)
+
+
+def decode(code):
+    steps = code.astype(jnp.int32).astype(jnp.float32)
+    value = jnp.exp2((steps + float(MID_CODE)) * (-1.0 / SCALE))
+    return jnp.where(steps >= TOP_CODE - MID_CODE, 0.0, value)
+
+
+def march_kernel(
+    ranks,
+    tiles,
+    entries,
+    position_ref,
+    table_ref,
+    index_ref,
+    volume_ref,
+    out_ref,
+    padded,
+    slab,
+    lookup,
+    order,
+    step_x,
+    rim_x,
+    step_y,
+    spread,
+    grad_x,
+    grad_y,
+    chosen,
+    params,
+    outbox,
+    inbox,
+    load_sem,
+    halo_send,
+    halo_recv,
+    send_sem,
+    recv_sem,
+    own_sem,
+):
+    depth_count, height, width = volume_ref.shape
+    cells = index_ref.shape[1]
+    piece = height // ranks
+    half = ranks // 2
+    me = lax.axis_index("depth")
+    tile = lax.axis_index("tile")
+    col_bit = lax.rem(tile, 2)
+    row_bit = lax.div(tile, 2)
+    col_partner = tile + 1 - 2 * col_bit
+    row_partner = lax.rem(tile + 2, tiles)
+    local = lax.rem(me, half)
+    side = lax.div(me, half)
+
+    load = pltpu.make_async_copy(volume_ref, padded.at[:, pl.ds(ROWS, height), :], load_sem)
+    load.start()
+
+    barrier = pltpu.get_barrier_semaphore()
+
+    def greet(apart, carry):
+        other = lax.rem(me + apart, ranks)
+        pl.semaphore_signal(barrier, inc=1, device_id=(other, tile), device_id_type=MESH)
+        return carry
+
+    lax.fori_loop(1, ranks, greet, 0)
+    pl.semaphore_signal(barrier, inc=1, device_id=(me, col_partner), device_id_type=MESH)
+    pl.semaphore_signal(barrier, inc=1, device_id=(me, row_partner), device_id_type=MESH)
+    pl.semaphore_wait(barrier, ranks + 1)
+
+    edge_row = pl.multiple_of((1 - row_bit) * (height - ROWS), ROWS)
+    edge_col = pl.multiple_of((1 - col_bit) * (width - LANES), LANES)
+    blank_row = pl.multiple_of(row_bit * (height + ROWS), ROWS)
+    got_row = pl.multiple_of((1 - row_bit) * (height + ROWS), ROWS)
+    send_row = pltpu.make_async_remote_copy(
+        src_ref=volume_ref.at[:, pl.ds(edge_row, ROWS), :],
+        dst_ref=padded.at[:, pl.ds(blank_row, ROWS), :],
+        send_sem=halo_send.at[0],
+        recv_sem=halo_recv.at[0],
+        device_id=(me, row_partner),
+        device_id_type=MESH,
+    )
+    send_row.start()
+    send_col = pltpu.make_async_remote_copy(
+        src_ref=volume_ref.at[:, :, pl.ds(edge_col, LANES)],
+        dst_ref=slab,
+        send_sem=halo_send.at[1],
+        recv_sem=halo_recv.at[1],
+        device_id=(me, col_partner),
+        device_id_type=MESH,
+    )
+    send_col.start()
+    padded[:, pl.ds(blank_row, ROWS), :] = jnp.zeros((depth_count, ROWS, width), jnp.bfloat16)
+
+    for place in range(ranks):
+        found = jnp.int32(0)
+        for rank in range(ranks):
+            found = jnp.where(position_ref[rank] == place, rank, found)
+        order[place] = found
+
+    def half_steps(plus, minus, shape):
+        return jnp.where(plus, 0.5, jnp.where(minus, -0.5, jnp.zeros(shape, jnp.float32))).astype(jnp.bfloat16)
+
+    from_col = lax.broadcasted_iota(jnp.int32, (width, width), 0)
+    to_col = lax.broadcasted_iota(jnp.int32, (width, width), 1)
+    step_x[...] = half_steps(from_col == to_col + 1, from_col == to_col - 1, (width, width))
+    rim_from = lax.broadcasted_iota(jnp.int32, (LANES, width), 0)
+    rim_to = lax.broadcasted_iota(jnp.int32, (LANES, width), 1)
+    right_to = (1 - col_bit) * width - 1
+    left_to = (col_bit - 1) * width
+    rim_x[...] = half_steps(
+        jnp.logical_and(rim_from == 0, rim_to == right_to),
+        jnp.logical_and(rim_from == LANES - 1, rim_to == left_to),
+        (LANES, width),
+    )
+    out_row = lax.broadcasted_iota(jnp.int32, (piece, piece + 2 * ROWS), 0) + ROWS
+    in_row = lax.broadcasted_iota(jnp.int32, (piece, piece + 2 * ROWS), 1)
+    step_y[...] = half_steps(in_row == out_row + 1, in_row == out_row - 1, (piece, piece + 2 * ROWS))
+    cell_of = lax.rem(rim_from, cells)
+    hit = jnp.logical_and(cell_of == lax.div(rim_to, CELL), rim_from < PARTS * cells)
+    spread[...] = jnp.where(hit, 1.0, 0.0).astype(jnp.bfloat16)
+
+    groups = LANES // cells
+
+    def arrange(step, carry):
+        index = index_ref[step]
+        wide = jnp.concatenate([index + group * entries for group in range(groups)], axis=0)
+        lookup[step] = wide.T
+        return carry
+
+    lax.fori_loop(0, depth_count, arrange, 0)
+
+    load.wait()
+    send_row.wait_send()
+    send_col.wait_send()
+    pltpu.make_async_remote_copy(
+        src_ref=volume_ref.at[:, pl.ds(edge_row, ROWS), :],
+        dst_ref=padded.at[:, pl.ds(got_row, ROWS), :],
+        send_sem=halo_send.at[0],
+        recv_sem=halo_recv.at[0],
+        device_id=(me, row_partner),
+        device_id_type=MESH,
+    ).wait_recv()
+    send_col.wait_recv()
+
+    shade_x = 0.6 * math.sqrt(0.7)
+    shade_y = 0.8 * math.sqrt(0.7)
+    param_count = table_ref.shape[0]
+    span = 2 * LANES
+
+    def target(turn):
+        far = (1 - side) * half + lax.rem(local + turn, half)
+        near = side * half + lax.rem(local + turn - half + 1 + half, half)
+        return jnp.where(turn < half, far, near)
+
+    def post(turn, there):
+        return pltpu.make_async_remote_copy(
+            src_ref=outbox.at[turn],
+            dst_ref=inbox.at[me],
+            send_sem=send_sem.at[turn],
+            recv_sem=recv_sem.at[me],
+            device_id=(there, tile),
+            device_id_type=MESH,
+        )
+
+    def block(turn, carry):
+        there = target(turn)
+        first = pl.multiple_of(there * piece, ROWS)
+
+        def slopes(step, carry):
+            window = padded[step, pl.ds(first, piece + 2 * ROWS), :]
+            grad_y[step] = jnp.dot(step_y[...], window, preferred_element_type=jnp.float32)
+            centre = padded[step, pl.ds(pl.multiple_of(first + ROWS, ROWS), piece), :]
+            rim = slab[step, pl.ds(first, piece), :]
+            inner = jnp.dot(centre, step_x[...], preferred_element_type=jnp.float32)
+            outer = jnp.dot(rim, rim_x[...], preferred_element_type=jnp.float32)
+            grad_x[step] = inner + outer
+            return carry
+
+        lax.fori_loop(0, depth_count, slopes, 0)
+
+        def chunk(part, carry):
+            row = pl.multiple_of(part * ROWS, ROWS)
+            at = pl.multiple_of(first + part * ROWS, ROWS)
+
+            def choose(step, carry):
+                index = lookup[step, pl.ds(at, ROWS), :]
+                for param in range(param_count):
+                    table = jnp.broadcast_to(table_ref[param : param + 1, :], (ROWS, LANES))
+                    value = jnp.take_along_axis(table, index, axis=1, mode="promise_in_bounds")
+                    place = pl.multiple_of((step * param_count + param) * ROWS, ROWS)
+                    chosen[pl.ds(place, ROWS), :] = value.astype(jnp.bfloat16)
+                return carry
+
+            lax.fori_loop(0, depth_count, choose, 0, unroll=2)
+            params[...] = jnp.dot(chosen[...], spread[...], preferred_element_type=jnp.float32)
+
+            for left in range(0, width, span):
+                cols = pl.ds(left, span)
+
+                def sample(step, carry):
+                    red, green, blue, trans = carry
+                    value = padded[step, pl.ds(pl.multiple_of(at + ROWS, ROWS), ROWS), cols].astype(jnp.float32)
+                    gx = grad_x[step, pl.ds(row, ROWS), cols]
+                    gy = grad_y[step, pl.ds(row, ROWS), cols]
+
+                    def param(number):
+                        place = pl.multiple_of((step * param_count + number) * ROWS, ROWS)
+                        return params[pl.ds(place, ROWS), cols]
+
+                    energy = gx * gx + gy * gy
+                    facing = shade_x * gx + shade_y * gy
+                    shade = 0.3 + facing * facing / (1.0 + energy)
+                    scaled = param(0) * value - param(1)
+                    keep = jnp.exp2(-(jnp.exp2(param(2) - scaled * scaled) * energy))
+                    weight = trans * (1.0 - keep) * shade
+                    return (
+                        red + weight * param(3),
+                        green + weight * param(4),
+                        blue + weight * param(5),
+                        trans * keep,
+                    )
+
+                zero = jnp.zeros((ROWS, span), jnp.float32)
+                start = (zero, zero, zero, zero + 1.0)
+                red, green, blue, trans = lax.fori_loop(0, depth_count, sample, start, unroll=3)
+                for channel, image in enumerate((red, green, blue, 1.0 - trans)):
+                    outbox[turn, channel, pl.ds(row, ROWS), cols] = encode(image)
+            return carry
+
+        lax.fori_loop(0, piece // ROWS, chunk, 0)
+
+        @pl.when(turn < ranks - 1)
+        def _():
+            post(turn, there).start()
+
+        return carry
+
+    lax.fori_loop(0, ranks, block, 0)
+    own = pltpu.make_async_copy(outbox.at[ranks - 1], inbox.at[me], own_sem)
+    own.start()
+    own.wait()
+
+    def settle(turn, carry):
+        there = target(turn)
+        post(turn, there).wait_send()
+        pltpu.make_async_remote_copy(
+            src_ref=outbox.at[turn],
+            dst_ref=inbox.at[there],
+            send_sem=send_sem.at[turn],
+            recv_sem=recv_sem.at[there],
+            device_id=(there, tile),
+            device_id_type=MESH,
+        ).wait_recv()
+        return carry
+
+    lax.fori_loop(0, ranks - 1, settle, 0)
+
+    def merge(part, carry):
+        rows = pl.ds(pl.multiple_of(part * ROWS, ROWS), ROWS)
+        for left in range(0, width, span):
+            cols = pl.ds(left, span)
+
+            def layer(place, images):
+                rank = order[place]
+                clear = 1.0 - images[3]
+                return tuple(images[c] + clear * decode(inbox[rank, c, rows, cols]) for c in range(4))
+
+            zero = jnp.zeros((ROWS, span), jnp.float32)
+            images = lax.fori_loop(0, ranks, layer, (zero,) * 4, unroll=2)
+            for c in range(4):
+                out_ref[c, rows, cols] = images[c]
+        return carry
+
+    lax.fori_loop(0, piece // ROWS, merge, 0)
+
+
+def split_tables(tables):
+    parts = []
+    rest = tables
+    for _ in range(PARTS):
+        part = lax.reduce_precision(rest, 8, 7)
+        parts.append(part)
+        rest = rest - part
+    wide = jnp.concatenate(parts, axis=1)
+    return jnp.pad(wide, ((0, 0), (0, LANES - wide.shape[1])))
+
+
+def fused_device(ranks, tiles, volume, table_index, brick_position, tf_center, tf_width, tf_peak, tf_color):
+    samples = volume[:, 0]
+    index = jnp.swapaxes(table_index[:, 0], 1, 2)
+    depth_count, height, width = samples.shape
+    piece = height // ranks
+    gain = math.sqrt(0.5 * LOG2E) / tf_width
+    level = jnp.log2(tf_peak * (LOG2E / (depth_count * ranks)))
+    tables = jnp.concatenate([gain[None], (gain * tf_center)[None], level[None], tf_color], axis=0)
+    param_count = tables.shape[0]
+    image = pl.pallas_call(
+        functools.partial(march_kernel, ranks, tiles, tf_center.shape[0]),
+        out_shape=jax.ShapeDtypeStruct((4, piece, width), jnp.float32),
+        in_specs=[
+            pl.BlockSpec(memory_space=pltpu.SMEM),
+            pl.BlockSpec(memory_space=pltpu.VMEM),
+            pl.BlockSpec(memory_space=pltpu.VMEM),
+            pl.BlockSpec(memory_space=pl.ANY),
+        ],
+        out_specs=pl.BlockSpec(memory_space=pltpu.VMEM),
+        scratch_shapes=[
+            pltpu.VMEM((depth_count, height + 2 * ROWS, width), jnp.bfloat16),
+            pltpu.VMEM((depth_count, height, LANES), jnp.bfloat16),
+            pltpu.VMEM((depth_count, height, LANES), jnp.int32),
+            pltpu.SMEM((ranks,), jnp.int32),
+            pltpu.VMEM((width, width), jnp.bfloat16),
+            pltpu.VMEM((LANES, width), jnp.bfloat16),
+            pltpu.VMEM((piece, piece + 2 * ROWS), jnp.bfloat16),
+            pltpu.VMEM((LANES, width), jnp.bfloat16),
+            pltpu.VMEM((depth_count, piece, width), jnp.float32),
+            pltpu.VMEM((depth_count, piece, width), jnp.float32),
+            pltpu.VMEM((depth_count * param_count * ROWS, LANES), jnp.bfloat16),
+            pltpu.VMEM((depth_count * param_count * ROWS, width), jnp.float32),
+            pltpu.VMEM((ranks, 4, piece, width), jnp.int16),
+            pltpu.VMEM((ranks, 4, piece, width), jnp.int16),
+            pltpu.SemaphoreType.DMA,
+            pltpu.SemaphoreType.DMA((2,)),
+            pltpu.SemaphoreType.DMA((2,)),
+            pltpu.SemaphoreType.DMA((ranks,)),
+            pltpu.SemaphoreType.DMA((ranks,)),
+            pltpu.SemaphoreType.DMA,
+        ],
+        compiler_params=pltpu.CompilerParams(
+            collective_id=0, has_side_effects=True, vmem_limit_bytes=56 * 1024 * 1024
+        ),
+    )(brick_position, split_tables(tables), index, samples)
+    return image[:, None]
 
 
 def from_partner(value, axis, apart):
@@ -90,19 +439,26 @@
     return image[:, None]
 
 
+def fits(ranks, tiles, shape):
+    height, width = shape[2], shape[3]
+    even = ranks % 2 == 0 and tiles == 4 and height % ranks == 0
+    return even and (height // ranks) % ROWS == 0 and width % (2 * LANES) == 0 and height % LANES == 0
+
+
 def solution(mesh):
-    return jax.shard_map(
-        on_device,
-        mesh=mesh,
-        in_specs=(
-            P("depth", "tile", None, None),
-            P("depth", "tile", None, None),
-            P(),
-            P(),
-            P(),
-            P(),
-            P(),
-        ),
-        out_specs=P(None, "tile", "depth", None),
-        check_vma=False,
-    )
+    ranks = mesh.shape["depth"]
+    tiles = mesh.shape["tile"]
+
+    def program(volume, *rest):
+        chosen = on_device
+        if fits(ranks, tiles, volume.shape):
+            chosen = functools.partial(fused_device, ranks, tiles)
+        return jax.shard_map(
+            chosen,
+            mesh=mesh,
+            in_specs=(P("depth", "tile", None, None), P("depth", "tile", None, None), P(), P(), P(), P(), P()),
+            out_specs=P(None, "tile", "depth", None),
+            check_vma=False,
+        )(volume, *rest)
+
+    return program

time: 376 us -> 123 us (0.33)
  waiting for transfers between devices: 138 us -> 0 us
  other arithmetic: 126 us -> 2.71 us
  Pallas kernels: 0 us -> 118 us
  local copies, waits for them, and re-layouts: 97.7 us -> 2.06 us
  starting transfers between devices: 9.5 us -> 0 us
    all_to_all x1 -> x0, waiting for transfers between devices: 137 us -> none  [on_device(): lax.all_to_all(partial_value, 'depth', split_axis=1, concat_axis=0, tiled...]
    pallas_call x0 -> x1, Pallas kernels: none -> 118 us  [fused_device(): pl.pallas_call(functools.partial(march_kernel, ranks, tiles, tf_center.sh...]
    while x86 -> x0, local copies, waits for them, and re-layouts: 36.2 us -> none
    convert_element_type x24 -> x0, other arithmetic: 30.8 us -> none  [the longest x12 15.7 us: sample(): lax.dynamic_index_in_dim(tall_pad, step, 0, keepdims=False)]
    mul x27 -> x0, other arithmetic: 26.4 us -> none  [the longest x12 22.4 us: light_sample(): trans = trans * keep]
    unnamed x19 -> x1, local copies, waits for them, and re-layouts: 27.4 us -> 2.06 us
    add x15 -> x0, other arithmetic: 24.1 us -> none  [the longest x12 21.8 us: light_sample(): rgb = rgb + weight[None] * params[3:6] * shade[None]]
    concatenate x3 -> x1, other arithmetic: 24.1 us -> 0.67 us  [split_tables(): wide = jnp.concatenate(parts, axis=1)]
  transfers between devices with their start and end apart: 3 -> 0, of which waited for: 2 -> 0; matrix products, arithmetic and copies ran while one was open for 7% -> 0% of each run, Pallas kernels for 0% -> 0%
where the time goes in v1:
time: 123 us
  Pallas kernels  118 us (96%)
  other arithmetic  2.71 us (2%)
  local copies, waits for them, and re-layouts  2.06 us (2%)
    pallas_call x1, Pallas kernels, fused_device(): pl.pallas_call(functools.partial(march_kernel, ranks, tiles, tf_center.sh...  118 us

profile of v1, /device:TPU:0, one launch (start us, length us, event | category | flops | bytes accessed | tf_op | source)
XLA Modules:
  0.0 123.0 jit_solution(11212156437040360674)
XLA Ops:
  0.0 0.7 multiply_bitcast_fusion
  0.7 0.7 multiply_bitcast_fusion.1
  1.3 0.7 fusion.1
  2.0 0.7 select_maximum_fusion.table_ref
  2.7 118.2 %shard_map.73 = f32[4,96,512]{2,1,0:T(8,128)} custom-call(s32[8]{0:T(128)} %position_ref.1, f32[6,128]{1,0:T(8,128)} %select_maximum_fusion.table_ref, s32[12,32,768]{2,1,0:T(8,128)} %bitcast.14, bf16[12,768,512]{2,1,0:T(8,128)(2,1)} %bitcast.12), custom_call_target="tpu_custom_call" | custom-call | tf_op jit(solution)/shard_map/pallas_call | solution.py:319
  120.9 2.1 %copy.10 = f32[4,1,96,512]{3,2,1,0:T(8,128)} copy(f32[4,1,96,512]{3,2,1,0:T(8,128)} %bitcast.13) | data formatting | bytes 1572864

commit v2 on v1

--- a/solution.py
+++ b/solution.py
@@ -15,7 +15,6 @@
 MID_CODE = 32768
 SCALE = TOP_CODE / OCTAVES
 LOG2E = 1.0 / math.log(2.0)
-PARTS = 3
 MESH = pl.DeviceIdType.MESH
 
 
@@ -34,9 +33,11 @@
 def march_kernel(
     ranks,
     tiles,
-    entries,
     position_ref,
-    table_ref,
+    center_ref,
+    width_ref,
+    peak_ref,
+    color_ref,
     index_ref,
     volume_ref,
     out_ref,
@@ -47,11 +48,9 @@
     step_x,
     rim_x,
     step_y,
-    spread,
+    tables,
     grad_x,
     grad_y,
-    chosen,
-    params,
     outbox,
     inbox,
     load_sem,
@@ -137,15 +136,20 @@
     out_row = lax.broadcasted_iota(jnp.int32, (piece, piece + 2 * ROWS), 0) + ROWS
     in_row = lax.broadcasted_iota(jnp.int32, (piece, piece + 2 * ROWS), 1)
     step_y[...] = half_steps(in_row == out_row + 1, in_row == out_row - 1, (piece, piece + 2 * ROWS))
-    cell_of = lax.rem(rim_from, cells)
-    hit = jnp.logical_and(cell_of == lax.div(rim_to, CELL), rim_from < PARTS * cells)
-    spread[...] = jnp.where(hit, 1.0, 0.0).astype(jnp.bfloat16)
+    entries = center_ref.shape[1]
+    gain = math.sqrt(0.5 * LOG2E) / width_ref[...]
+    level = jnp.log(peak_ref[...] * (LOG2E / (depth_count * ranks))) * LOG2E
+    tables[...] = jnp.zeros(tables.shape, jnp.float32)
+    tables[0:1, 0:entries] = gain
+    tables[1:2, 0:entries] = gain * center_ref[...]
+    tables[2:3, 0:entries] = level
+    tables[3:6, 0:entries] = color_ref[...]
 
     groups = LANES // cells
 
     def arrange(step, carry):
         index = index_ref[step]
-        wide = jnp.concatenate([index + group * entries for group in range(groups)], axis=0)
+        wide = jnp.concatenate([index] * groups, axis=0)
         lookup[step] = wide.T
         return carry
 
@@ -166,8 +170,8 @@
 
     shade_x = 0.6 * math.sqrt(0.7)
     shade_y = 0.8 * math.sqrt(0.7)
-    param_count = table_ref.shape[0]
-    span = 2 * LANES
+    cell_pattern = lax.div(lax.broadcasted_iota(jnp.int32, (ROWS, LANES), 1), CELL)
+    cells_across = LANES // CELL
 
     def target(turn):
         far = (1 - side) * half + lax.rem(local + turn, half)
@@ -191,47 +195,40 @@
         def slopes(step, carry):
             window = padded[step, pl.ds(first, piece + 2 * ROWS), :]
             grad_y[step] = jnp.dot(step_y[...], window, preferred_element_type=jnp.float32)
-            centre = padded[step, pl.ds(pl.multiple_of(first + ROWS, ROWS), piece), :]
-            rim = slab[step, pl.ds(first, piece), :]
-            inner = jnp.dot(centre, step_x[...], preferred_element_type=jnp.float32)
-            outer = jnp.dot(rim, rim_x[...], preferred_element_type=jnp.float32)
-            grad_x[step] = inner + outer
             return carry
 
-        lax.fori_loop(0, depth_count, slopes, 0)
+        lax.fori_loop(0, depth_count, slopes, 0, unroll=2)
+        centre = padded[:, pl.ds(pl.multiple_of(first + ROWS, ROWS), piece), :].reshape(depth_count * piece, width)
+        rim = slab[:, pl.ds(first, piece), :].reshape(depth_count * piece, LANES)
+        inner = jnp.dot(centre, step_x[...], preferred_element_type=jnp.float32)
+        outer = jnp.dot(rim, rim_x[...], preferred_element_type=jnp.float32)
+        grad_x[...] = (inner + outer).reshape(depth_count, piece, width)
 
         def chunk(part, carry):
             row = pl.multiple_of(part * ROWS, ROWS)
             at = pl.multiple_of(first + part * ROWS, ROWS)
-
-            def choose(step, carry):
-                index = lookup[step, pl.ds(at, ROWS), :]
-                for param in range(param_count):
-                    table = jnp.broadcast_to(table_ref[param : param + 1, :], (ROWS, LANES))
-                    value = jnp.take_along_axis(table, index, axis=1, mode="promise_in_bounds")
-                    place = pl.multiple_of((step * param_count + param) * ROWS, ROWS)
-                    chosen[pl.ds(place, ROWS), :] = value.astype(jnp.bfloat16)
-                return carry
-
-            lax.fori_loop(0, depth_count, choose, 0, unroll=2)
-            params[...] = jnp.dot(chosen[...], spread[...], preferred_element_type=jnp.float32)
-
-            for left in range(0, width, span):
-                cols = pl.ds(left, span)
+            rows = [jnp.broadcast_to(tables[p : p + 1, :], (ROWS, LANES)) for p in range(6)]
+
+            for left in range(0, width, LANES):
+                cols = pl.ds(left, LANES)
+                pattern = cell_pattern + left // LANES * cells_across
 
                 def sample(step, carry):
                     red, green, blue, trans = carry
                     value = padded[step, pl.ds(pl.multiple_of(at + ROWS, ROWS), ROWS), cols].astype(jnp.float32)
                     gx = grad_x[step, pl.ds(row, ROWS), cols]
                     gy = grad_y[step, pl.ds(row, ROWS), cols]
+                    cell = lookup[step, pl.ds(at, ROWS), :]
+                    index = jnp.take_along_axis(cell, pattern, axis=1, mode="promise_in_bounds")
 
                     def param(number):
-                        place = pl.multiple_of((step * param_count + number) * ROWS, ROWS)
-                        return params[pl.ds(place, ROWS), cols]
+                        return jnp.take_along_axis(rows[number], index, axis=1, mode="promise_in_bounds")
 
                     energy = gx * gx + gy * gy
                     facing = shade_x * gx + shade_y * gy
-                    shade = 0.3 + facing * facing / (1.0 + energy)
+                    base = 1.0 + energy
+                    rough = pl.reciprocal(base, approx=True)
+                    shade = 0.3 + facing * facing * (rough * (2.0 - base * rough))
                     scaled = param(0) * value - param(1)
                     keep = jnp.exp2(-(jnp.exp2(param(2) - scaled * scaled) * energy))
                     weight = trans * (1.0 - keep) * shade
@@ -242,9 +239,9 @@
                         trans * keep,
                     )
 
-                zero = jnp.zeros((ROWS, span), jnp.float32)
+                zero = jnp.zeros((ROWS, LANES), jnp.float32)
                 start = (zero, zero, zero, zero + 1.0)
-                red, green, blue, trans = lax.fori_loop(0, depth_count, sample, start, unroll=3)
+                red, green, blue, trans = lax.fori_loop(0, depth_count, sample, start, unroll=6)
                 for channel, image in enumerate((red, green, blue, 1.0 - trans)):
                     outbox[turn, channel, pl.ds(row, ROWS), cols] = encode(image)
             return carry
@@ -277,6 +274,8 @@
 
     lax.fori_loop(0, ranks - 1, settle, 0)
 
+    span = 2 * LANES
+
     def merge(part, carry):
         rows = pl.ds(pl.multiple_of(part * ROWS, ROWS), ROWS)
         for left in range(0, width, span):
@@ -296,31 +295,19 @@
     lax.fori_loop(0, piece // ROWS, merge, 0)
 
 
-def split_tables(tables):
-    parts = []
-    rest = tables
-    for _ in range(PARTS):
-        part = lax.reduce_precision(rest, 8, 7)
-        parts.append(part)
-        rest = rest - part
-    wide = jnp.concatenate(parts, axis=1)
-    return jnp.pad(wide, ((0, 0), (0, LANES - wide.shape[1])))
-
-
 def fused_device(ranks, tiles, volume, table_index, brick_position, tf_center, tf_width, tf_peak, tf_color):
     samples = volume[:, 0]
     index = jnp.swapaxes(table_index[:, 0], 1, 2)
     depth_count, height, width = samples.shape
     piece = height // ranks
-    gain = math.sqrt(0.5 * LOG2E) / tf_width
-    level = jnp.log2(tf_peak * (LOG2E / (depth_count * ranks)))
-    tables = jnp.concatenate([gain[None], (gain * tf_center)[None], level[None], tf_color], axis=0)
-    param_count = tables.shape[0]
     image = pl.pallas_call(
-        functools.partial(march_kernel, ranks, tiles, tf_center.shape[0]),
+        functools.partial(march_kernel, ranks, tiles),
         out_shape=jax.ShapeDtypeStruct((4, piece, width), jnp.float32),
         in_specs=[
             pl.BlockSpec(memory_space=pltpu.SMEM),
+            pl.BlockSpec(memory_space=pltpu.VMEM),
+            pl.BlockSpec(memory_space=pltpu.VMEM),
+            pl.BlockSpec(memory_space=pltpu.VMEM),
             pl.BlockSpec(memory_space=pltpu.VMEM),
             pl.BlockSpec(memory_space=pltpu.VMEM),
             pl.BlockSpec(memory_space=pl.ANY),
@@ -334,11 +321,9 @@
             pltpu.VMEM((width, width), jnp.bfloat16),
             pltpu.VMEM((LANES, width), jnp.bfloat16),
             pltpu.VMEM((piece, piece + 2 * ROWS), jnp.bfloat16),
-            pltpu.VMEM((LANES, width), jnp.bfloat16),
+            pltpu.VMEM((8, LANES), jnp.float32),
             pltpu.VMEM((depth_count, piece, width), jnp.float32),
             pltpu.VMEM((depth_count, piece, width), jnp.float32),
-            pltpu.VMEM((depth_count * param_count * ROWS, LANES), jnp.bfloat16),
-            pltpu.VMEM((depth_count * param_count * ROWS, width), jnp.float32),
             pltpu.VMEM((ranks, 4, piece, width), jnp.int16),
             pltpu.VMEM((ranks, 4, piece, width), jnp.int16),
             pltpu.SemaphoreType.DMA,
@@ -351,7 +336,7 @@
         compiler_params=pltpu.CompilerParams(
             collective_id=0, has_side_effects=True, vmem_limit_bytes=56 * 1024 * 1024
         ),
-    )(brick_position, split_tables(tables), index, samples)
+    )(brick_position, tf_center[None], tf_width[None], tf_peak[None], tf_color, index, samples)
     return image[:, None]
 
 

time: 123 us -> 160 us (1.30)
  Pallas kernels: 118 us -> 157 us
  other arithmetic: 2.71 us -> 0 us
    pallas_call x1, Pallas kernels: 118 us -> 157 us  [fused_device(): pl.pallas_call(functools.partial(march_kernel, ranks, tiles), out_shape=j...]
where the time goes in v2:
time: 160 us
  Pallas kernels  157 us (98%)
  local copies, waits for them, and re-layouts  2.06 us (1%)
    pallas_call x1, Pallas kernels, fused_device(): pl.pallas_call(functools.partial(march_kernel, ranks, tiles), out_shape=j...  157 us

profile of v2, /device:TPU:0, one launch (start us, length us, event | category | flops | bytes accessed | tf_op | source)
XLA Modules:
  0.0 159.6 jit_solution(13158168792002641419)
XLA Ops:
  0.0 157.5 %shard_map.73 = f32[4,96,512]{2,1,0:T(8,128)} custom-call(s32[8]{0:T(128)} %position_ref.1, f32[1,16]{1,0:T(1,128)} %bitcast.13, f32[1,16]{1,0:T(1,128)} %bitcast.14, f32[1,16]{1,0:T(1,128)} %bitcast.15, f32[3,16]{1,0:T(4,128)} %color_ref.1, s32[12,32,768]{2,1,0:T(8,128)} %bitcast.12, bf16[12,768,512]{2,1,0:T(8,128)(2,1)} %bitcast.10), custom_call_target="tpu_custom_call" | custom-call | tf_op jit(solution)/shard_map/pallas_call | solution.py:303
  157.5 2.1 %copy.10 = f32[4,1,96,512]{3,2,1,0:T(8,128)} copy(f32[4,1,96,512]{3,2,1,0:T(8,128)} %bitcast.11) | data formatting | bytes 1572864

commit v3 on v2

--- a/solution.py
+++ b/solution.py
@@ -10,6 +10,7 @@
 CELL = 16
 ROWS = 16
 LANES = 128
+RIM = 8
 OCTAVES = 30.0
 TOP_CODE = 65535.0
 MID_CODE = 32768
@@ -43,14 +44,15 @@
     out_ref,
     padded,
     slab,
-    lookup,
     order,
-    step_x,
-    rim_x,
+    half_eye,
+    rim_pick,
     step_y,
     tables,
-    grad_x,
+    turned,
     grad_y,
+    cell_params,
+    image_turned,
     outbox,
     inbox,
     load_sem,
@@ -62,6 +64,8 @@
 ):
     depth_count, height, width = volume_ref.shape
     cells = index_ref.shape[1]
+    span = half_eye.shape[0]
+    window = step_y.shape[0]
     piece = height // ranks
     half = ranks // 2
     me = lax.axis_index("depth")
@@ -70,7 +74,6 @@
     row_bit = lax.div(tile, 2)
     col_partner = tile + 1 - 2 * col_bit
     row_partner = lax.rem(tile + 2, tiles)
-    local = lax.rem(me, half)
     side = lax.div(me, half)
 
     load = pltpu.make_async_copy(volume_ref, padded.at[:, pl.ds(ROWS, height), :], load_sem)
@@ -118,42 +121,31 @@
             found = jnp.where(position_ref[rank] == place, rank, found)
         order[place] = found
 
-    def half_steps(plus, minus, shape):
-        return jnp.where(plus, 0.5, jnp.where(minus, -0.5, jnp.zeros(shape, jnp.float32))).astype(jnp.bfloat16)
-
-    from_col = lax.broadcasted_iota(jnp.int32, (width, width), 0)
-    to_col = lax.broadcasted_iota(jnp.int32, (width, width), 1)
-    step_x[...] = half_steps(from_col == to_col + 1, from_col == to_col - 1, (width, width))
-    rim_from = lax.broadcasted_iota(jnp.int32, (LANES, width), 0)
-    rim_to = lax.broadcasted_iota(jnp.int32, (LANES, width), 1)
-    right_to = (1 - col_bit) * width - 1
-    left_to = (col_bit - 1) * width
-    rim_x[...] = half_steps(
-        jnp.logical_and(rim_from == 0, rim_to == right_to),
-        jnp.logical_and(rim_from == LANES - 1, rim_to == left_to),
-        (LANES, width),
-    )
-    out_row = lax.broadcasted_iota(jnp.int32, (piece, piece + 2 * ROWS), 0) + ROWS
-    in_row = lax.broadcasted_iota(jnp.int32, (piece, piece + 2 * ROWS), 1)
-    step_y[...] = half_steps(in_row == out_row + 1, in_row == out_row - 1, (piece, piece + 2 * ROWS))
+    def from_mask(mask, number):
+        return jnp.where(mask, number, 0.0).astype(jnp.bfloat16)
+
+    eye_row = lax.broadcasted_iota(jnp.int32, (span, span), 0)
+    eye_col = lax.broadcasted_iota(jnp.int32, (span, span), 1)
+    half_eye[...] = from_mask(eye_row == eye_col, 0.5)
+    pick_row = lax.broadcasted_iota(jnp.int32, (ROWS, LANES), 0)
+    pick_col = lax.broadcasted_iota(jnp.int32, (ROWS, LANES), 1)
+    wanted_row = jnp.where(col_bit == 1, RIM - 1, RIM)
+    wanted_col = jnp.where(col_bit == 1, LANES - 1, 0)
+    rim_pick[...] = from_mask(jnp.logical_and(pick_row == wanted_row, pick_col == wanted_col), 0.5)
+    window_row = lax.broadcasted_iota(jnp.int32, (window, LANES), 0)
+    window_at = jnp.where(window_row < LANES, window_row, jnp.where(window_row < LANES + ROWS, window_row - LANES - ROWS, window_row - ROWS))
+    lane_at = lax.broadcasted_iota(jnp.int32, (window, LANES), 1)
+    plus = from_mask(window_at == lane_at + 1, 1.0)
+    step_y[...] = plus - from_mask(window_at == lane_at - 1, 1.0)
+
     entries = center_ref.shape[1]
     gain = math.sqrt(0.5 * LOG2E) / width_ref[...]
     level = jnp.log(peak_ref[...] * (LOG2E / (depth_count * ranks))) * LOG2E
     tables[...] = jnp.zeros(tables.shape, jnp.float32)
-    tables[0:1, 0:entries] = gain
+    tables[0:1, 0:entries] = gain + gain
     tables[1:2, 0:entries] = gain * center_ref[...]
     tables[2:3, 0:entries] = level
     tables[3:6, 0:entries] = color_ref[...]
-
-    groups = LANES // cells
-
-    def arrange(step, carry):
-        index = index_ref[step]
-        wide = jnp.concatenate([index] * groups, axis=0)
-        lookup[step] = wide.T
-        return carry
-
-    lax.fori_loop(0, depth_count, arrange, 0)
 
     load.wait()
     send_row.wait_send()
@@ -170,111 +162,124 @@
 
     shade_x = 0.6 * math.sqrt(0.7)
     shade_y = 0.8 * math.sqrt(0.7)
-    cell_pattern = lax.div(lax.broadcasted_iota(jnp.int32, (ROWS, LANES), 1), CELL)
-    cells_across = LANES // CELL
-
-    def target(turn):
-        far = (1 - side) * half + lax.rem(local + turn, half)
-        near = side * half + lax.rem(local + turn - half + 1 + half, half)
-        return jnp.where(turn < half, far, near)
-
-    def post(turn, there):
+    def post(there):
         return pltpu.make_async_remote_copy(
-            src_ref=outbox.at[turn],
+            src_ref=outbox.at[:, pl.ds(pl.multiple_of(there * piece, ROWS), piece), :],
             dst_ref=inbox.at[me],
-            send_sem=send_sem.at[turn],
+            send_sem=send_sem.at[there],
             recv_sem=recv_sem.at[me],
             device_id=(there, tile),
             device_id_type=MESH,
         )
 
+    blocks = height // LANES // 2
+    transposed = (((1,), (1,)), ((), ()))
+
     def block(turn, carry):
-        there = target(turn)
-        first = pl.multiple_of(there * piece, ROWS)
-
-        def slopes(step, carry):
-            window = padded[step, pl.ds(first, piece + 2 * ROWS), :]
-            grad_y[step] = jnp.dot(step_y[...], window, preferred_element_type=jnp.float32)
+        away = 1 - lax.div(turn, blocks)
+        part = lax.rem(turn, blocks)
+        area = lax.rem(side + away, 2)
+        first = pl.multiple_of((area * blocks + part) * LANES, LANES)
+        entry_rows = [jnp.broadcast_to(tables[p : p + 1, :], (cells, LANES)) for p in range(6)]
+
+        def prepare(step, carry):
+            index = index_ref[step, :, pl.ds(first, LANES)]
+            for p in range(6):
+                found = jnp.take_along_axis(entry_rows[p], index, axis=1, mode="promise_in_bounds")
+                cell_params[step, p * cells : (p + 1) * cells, :] = found
+            for left in range(0, width, span):
+                cols = pl.ds(left, span)
+                near = padded[step, pl.ds(pl.multiple_of(first + ROWS, ROWS), LANES), cols]
+                above = padded[step, pl.ds(first, ROWS), cols]
+                below = padded[step, pl.ds(pl.multiple_of(first + ROWS + LANES, ROWS), ROWS), cols]
+                rows = jnp.concatenate([near, above, below], axis=0)
+                flipped = lax.dot_general(half_eye[...], rows, transposed, preferred_element_type=jnp.float32)
+                turned[step, RIM + left : RIM + left + span, :] = flipped[:, :LANES]
+                grad_y[step, cols, :] = jnp.dot(
+                    flipped.astype(jnp.bfloat16), step_y[...], preferred_element_type=jnp.float32
+                )
+            rim = slab[step, pl.ds(first, LANES), :]
+            edges = lax.dot_general(rim_pick[...], rim, transposed, preferred_element_type=jnp.float32)
+            turned[step, 0:RIM, :] = edges[:RIM]
+            turned[step, RIM + width : 2 * RIM + width, :] = edges[RIM:]
             return carry
 
-        lax.fori_loop(0, depth_count, slopes, 0, unroll=2)
-        centre = padded[:, pl.ds(pl.multiple_of(first + ROWS, ROWS), piece), :].reshape(depth_count * piece, width)
-        rim = slab[:, pl.ds(first, piece), :].reshape(depth_count * piece, LANES)
-        inner = jnp.dot(centre, step_x[...], preferred_element_type=jnp.float32)
-        outer = jnp.dot(rim, rim_x[...], preferred_element_type=jnp.float32)
-        grad_x[...] = (inner + outer).reshape(depth_count, piece, width)
-
-        def chunk(part, carry):
-            row = pl.multiple_of(part * ROWS, ROWS)
-            at = pl.multiple_of(first + part * ROWS, ROWS)
-            rows = [jnp.broadcast_to(tables[p : p + 1, :], (ROWS, LANES)) for p in range(6)]
-
+        lax.fori_loop(0, depth_count, prepare, 0, unroll=2)
+
+        def column(cell, carry):
+            top = pl.multiple_of(cell * CELL, CELL)
+
+            def sample(step, carry):
+                red, green, blue, trans = carry
+                value = turned[step, pl.ds(top + RIM, CELL), :]
+                gx = turned[step, pl.ds(top + RIM + 1, CELL), :] - turned[step, pl.ds(top + RIM - 1, CELL), :]
+                gy = grad_y[step, pl.ds(top, CELL), :]
+
+                def param(number):
+                    row = cell_params[step, pl.ds(number * cells + cell, 1), :]
+                    return jnp.broadcast_to(row, (CELL, LANES))
+
+                energy = gx * gx + gy * gy
+                facing = shade_x * gx + shade_y * gy
+                base = 1.0 + energy
+                rough = pl.reciprocal(base, approx=True)
+                shade = 0.3 + facing * facing * (rough * (2.0 - base * rough))
+                scaled = param(0) * value - param(1)
+                keep = jnp.exp2(-(jnp.exp2(param(2) - scaled * scaled) * energy))
+                weight = trans * (1.0 - keep) * shade
+                return (
+                    red + weight * param(3),
+                    green + weight * param(4),
+                    blue + weight * param(5),
+                    trans * keep,
+                )
+
+            zero = jnp.zeros((CELL, LANES), jnp.float32)
+            start = (zero, zero, zero, zero + 1.0)
+            red, green, blue, trans = lax.fori_loop(0, depth_count, sample, start, unroll=True)
+            for channel, image in enumerate((red, green, blue, 1.0 - trans)):
+                image_turned[channel, pl.ds(top, CELL), :] = image
+            return carry
+
+        lax.fori_loop(0, cells, column, 0)
+
+        for channel in range(4):
             for left in range(0, width, LANES):
-                cols = pl.ds(left, LANES)
-                pattern = cell_pattern + left // LANES * cells_across
-
-                def sample(step, carry):
-                    red, green, blue, trans = carry
-                    value = padded[step, pl.ds(pl.multiple_of(at + ROWS, ROWS), ROWS), cols].astype(jnp.float32)
-                    gx = grad_x[step, pl.ds(row, ROWS), cols]
-                    gy = grad_y[step, pl.ds(row, ROWS), cols]
-                    cell = lookup[step, pl.ds(at, ROWS), :]
-                    index = jnp.take_along_axis(cell, pattern, axis=1, mode="promise_in_bounds")
-
-                    def param(number):
-                        return jnp.take_along_axis(rows[number], index, axis=1, mode="promise_in_bounds")
-
-                    energy = gx * gx + gy * gy
-                    facing = shade_x * gx + shade_y * gy
-                    base = 1.0 + energy
-                    rough = pl.reciprocal(base, approx=True)
-                    shade = 0.3 + facing * facing * (rough * (2.0 - base * rough))
-                    scaled = param(0) * value - param(1)
-                    keep = jnp.exp2(-(jnp.exp2(param(2) - scaled * scaled) * energy))
-                    weight = trans * (1.0 - keep) * shade
-                    return (
-                        red + weight * param(3),
-                        green + weight * param(4),
-                        blue + weight * param(5),
-                        trans * keep,
-                    )
-
-                zero = jnp.zeros((ROWS, LANES), jnp.float32)
-                start = (zero, zero, zero, zero + 1.0)
-                red, green, blue, trans = lax.fori_loop(0, depth_count, sample, start, unroll=6)
-                for channel, image in enumerate((red, green, blue, 1.0 - trans)):
-                    outbox[turn, channel, pl.ds(row, ROWS), cols] = encode(image)
+                flat = image_turned[channel, left : left + LANES, :].T
+                outbox[channel, pl.ds(first, LANES), left : left + LANES] = encode(flat)
+
+        def dispatch(number, carry):
+            there = area * half + number
+
+            @pl.when(there != me)
+            def _():
+                post(there).start()
+
             return carry
 
-        lax.fori_loop(0, piece // ROWS, chunk, 0)
-
-        @pl.when(turn < ranks - 1)
-        def _():
-            post(turn, there).start()
-
+        lax.fori_loop(part * LANES // piece, (part + 1) * LANES // piece, dispatch, 0)
         return carry
 
-    lax.fori_loop(0, ranks, block, 0)
-    own = pltpu.make_async_copy(outbox.at[ranks - 1], inbox.at[me], own_sem)
+    lax.fori_loop(0, 2 * blocks, block, 0)
+    mine = outbox.at[:, pl.ds(pl.multiple_of(me * piece, ROWS), piece), :]
+    own = pltpu.make_async_copy(mine, inbox.at[me], own_sem)
     own.start()
     own.wait()
 
-    def settle(turn, carry):
-        there = target(turn)
-        post(turn, there).wait_send()
+    def settle(apart, carry):
+        there = lax.rem(me + apart, ranks)
+        post(there).wait_send()
         pltpu.make_async_remote_copy(
-            src_ref=outbox.at[turn],
+            src_ref=mine,
             dst_ref=inbox.at[there],
-            send_sem=send_sem.at[turn],
+            send_sem=send_sem.at[there],
             recv_sem=recv_sem.at[there],
             device_id=(there, tile),
             device_id_type=MESH,
         ).wait_recv()
         return carry
 
-    lax.fori_loop(0, ranks - 1, settle, 0)
-
-    span = 2 * LANES
+    lax.fori_loop(1, ranks, settle, 0)
 
     def merge(part, carry):
         rows = pl.ds(pl.multiple_of(part * ROWS, ROWS), ROWS)
@@ -300,6 +305,7 @@
     index = jnp.swapaxes(table_index[:, 0], 1, 2)
     depth_count, height, width = samples.shape
     piece = height // ranks
+    cells = index.shape[1]
     image = pl.pallas_call(
         functools.partial(march_kernel, ranks, tiles),
         out_shape=jax.ShapeDtypeStruct((4, piece, width), jnp.float32),
@@ -316,15 +322,16 @@
         scratch_shapes=[
             pltpu.VMEM((depth_count, height + 2 * ROWS, width), jnp.bfloat16),
             pltpu.VMEM((depth_count, height, LANES), jnp.bfloat16),
-            pltpu.VMEM((depth_count, height, LANES), jnp.int32),
             pltpu.SMEM((ranks,), jnp.int32),
-            pltpu.VMEM((width, width), jnp.bfloat16),
-            pltpu.VMEM((LANES, width), jnp.bfloat16),
-            pltpu.VMEM((piece, piece + 2 * ROWS), jnp.bfloat16),
+            pltpu.VMEM((2 * LANES, 2 * LANES), jnp.bfloat16),
+            pltpu.VMEM((ROWS, LANES), jnp.bfloat16),
+            pltpu.VMEM((LANES + 2 * ROWS, LANES), jnp.bfloat16),
             pltpu.VMEM((8, LANES), jnp.float32),
-            pltpu.VMEM((depth_count, piece, width), jnp.float32),
-            pltpu.VMEM((depth_count, piece, width), jnp.float32),
-            pltpu.VMEM((ranks, 4, piece, width), jnp.int16),
+            pltpu.VMEM((depth_count, width + 2 * RIM, LANES), jnp.float32),
+            pltpu.VMEM((depth_count, width, LANES), jnp.float32),
+            pltpu.VMEM((depth_count, 6 * cells, LANES), jnp.float32),
+            pltpu.VMEM((4, width, LANES), jnp.float32),
+            pltpu.VMEM((4, height, width), jnp.int16),
             pltpu.VMEM((ranks, 4, piece, width), jnp.int16),
             pltpu.SemaphoreType.DMA,
             pltpu.SemaphoreType.DMA((2,)),
@@ -427,7 +434,7 @@
 def fits(ranks, tiles, shape):
     height, width = shape[2], shape[3]
     even = ranks % 2 == 0 and tiles == 4 and height % ranks == 0
-    return even and (height // ranks) % ROWS == 0 and width % (2 * LANES) == 0 and height % LANES == 0
+    return even and (height // ranks) % ROWS == 0 and width % (2 * LANES) == 0 and height % (2 * LANES) == 0
 
 
 def solution(mesh):

time: 160 us -> 103 us (0.64)
  the two profiles are of different devices: /device:TPU:0 before, /device:TPU:28 now
where the time goes in v3:
time: 103 us
  Pallas kernels  101 us (98%)
  local copies, waits for them, and re-layouts  2.06 us (2%)
    pallas_call x1, Pallas kernels, fused_device(): pl.pallas_call(functools.partial(march_kernel, ranks, tiles), out_shape=j...  101 us
    unnamed x1, local copies, waits for them, and re-layouts  2.06 us

profile of v3, /device:TPU:28, one launch (start us, length us, event | category | flops | bytes accessed | tf_op | source)
XLA Modules:
  0.0 103.1 jit_solution(9512715586275618789)
XLA Ops:
  0.0 101.0 %shard_map.73 = f32[4,96,512]{2,1,0:T(8,128)} custom-call(s32[8]{0:T(128)} %position_ref.1, f32[1,16]{1,0:T(1,128)} %bitcast.13, f32[1,16]{1,0:T(1,128)} %bitcast.14, f32[1,16]{1,0:T(1,128)} %bitcast.15, f32[3,16]{1,0:T(4,128)} %color_ref.1, s32[12,32,768]{2,1,0:T(8,128)} %bitcast.12, bf16[12,768,512]{2,1,0:T(8,128)(2,1)} %bitcast.10), custom_call_target="tpu_custom_call" | custom-call | tf_op jit(solution)/shard_map/pallas_call | solution.py:309
  101.0 2.1 %copy.10 = f32[4,1,96,512]{3,2,1,0:T(8,128)} copy(f32[4,1,96,512]{3,2,1,0:T(8,128)} %bitcast.11) | data formatting | bytes 1572864

commit v4 on v3

--- a/solution.py
+++ b/solution.py
@@ -162,12 +162,19 @@
 
     shade_x = 0.6 * math.sqrt(0.7)
     shade_y = 0.8 * math.sqrt(0.7)
-    def post(there):
+    unit = math.gcd(piece, LANES)
+    per_piece = piece // unit
+    per_block = LANES // unit
+
+    def post(segment):
+        there = lax.div(segment, per_piece)
+        rows = pl.multiple_of(segment * unit, ROWS)
+        inside = pl.multiple_of(lax.rem(segment, per_piece) * unit, ROWS)
         return pltpu.make_async_remote_copy(
-            src_ref=outbox.at[:, pl.ds(pl.multiple_of(there * piece, ROWS), piece), :],
-            dst_ref=inbox.at[me],
-            send_sem=send_sem.at[there],
-            recv_sem=recv_sem.at[me],
+            src_ref=outbox.at[:, pl.ds(rows, unit), :],
+            dst_ref=inbox.at[me, :, pl.ds(inside, unit), :],
+            send_sem=send_sem.at[segment],
+            recv_sem=recv_sem.at[me, lax.rem(segment, per_piece)],
             device_id=(there, tile),
             device_id_type=MESH,
         )
@@ -177,7 +184,7 @@
 
     def block(turn, carry):
         away = 1 - lax.div(turn, blocks)
-        part = lax.rem(turn, blocks)
+        part = lax.rem(turn + me, blocks)
         area = lax.rem(side + away, 2)
         first = pl.multiple_of((area * blocks + part) * LANES, LANES)
         entry_rows = [jnp.broadcast_to(tables[p : p + 1, :], (cells, LANES)) for p in range(6)]
@@ -249,15 +256,15 @@
                 outbox[channel, pl.ds(first, LANES), left : left + LANES] = encode(flat)
 
         def dispatch(number, carry):
-            there = area * half + number
-
-            @pl.when(there != me)
+            segment = (area * blocks + part) * per_block + number
+
+            @pl.when(lax.div(segment, per_piece) != me)
             def _():
-                post(there).start()
+                post(segment).start()
 
             return carry
 
-        lax.fori_loop(part * LANES // piece, (part + 1) * LANES // piece, dispatch, 0)
+        lax.fori_loop(0, per_block, dispatch, 0)
         return carry
 
     lax.fori_loop(0, 2 * blocks, block, 0)
@@ -266,20 +273,22 @@
     own.start()
     own.wait()
 
-    def settle(apart, carry):
-        there = lax.rem(me + apart, ranks)
-        post(there).wait_send()
+    def settle(number, carry):
+        there = lax.rem(me + 1 + lax.div(number, per_piece), ranks)
+        inside = lax.rem(number, per_piece)
+        post(there * per_piece + inside).wait_send()
+        rows = pl.ds(pl.multiple_of(inside * unit, ROWS), unit)
         pltpu.make_async_remote_copy(
-            src_ref=mine,
-            dst_ref=inbox.at[there],
-            send_sem=send_sem.at[there],
-            recv_sem=recv_sem.at[there],
+            src_ref=outbox.at[:, pl.ds(0, unit), :],
+            dst_ref=inbox.at[there, :, rows, :],
+            send_sem=send_sem.at[0],
+            recv_sem=recv_sem.at[there, inside],
             device_id=(there, tile),
             device_id_type=MESH,
         ).wait_recv()
         return carry
 
-    lax.fori_loop(1, ranks, settle, 0)
+    lax.fori_loop(0, (ranks - 1) * per_piece, settle, 0)
 
     def merge(part, carry):
         rows = pl.ds(pl.multiple_of(part * ROWS, ROWS), ROWS)
@@ -336,8 +345,8 @@
             pltpu.SemaphoreType.DMA,
             pltpu.SemaphoreType.DMA((2,)),
             pltpu.SemaphoreType.DMA((2,)),
-            pltpu.SemaphoreType.DMA((ranks,)),
-            pltpu.SemaphoreType.DMA((ranks,)),
+            pltpu.SemaphoreType.DMA((height // math.gcd(piece, LANES),)),
+            pltpu.SemaphoreType.DMA((ranks, piece // math.gcd(piece, LANES))),
             pltpu.SemaphoreType.DMA,
         ],
         compiler_params=pltpu.CompilerParams(

time: 103 us -> 102 us (level)
  the two profiles are of different devices: /device:TPU:28 before, /device:TPU:0 now
where the time goes in v4:
time: 102 us; the launch traced here: 100 us
  Pallas kernels  98.2 us (96%)
  local copies, waits for them, and re-layouts  2.06 us (2%)
    pallas_call x1, Pallas kernels, fused_device(): pl.pallas_call(functools.partial(march_kernel, ranks, tiles), out_shape=j...  98.2 us
    unnamed x1, local copies, waits for them, and re-layouts  2.06 us

profile of v4, /device:TPU:0, one launch (start us, length us, event | category | flops | bytes accessed | tf_op | source)
XLA Modules:
  0.0 100.3 jit_solution(2886113383464367969)
XLA Ops:
  0.0 98.2 %shard_map.73 = f32[4,96,512]{2,1,0:T(8,128)} custom-call(s32[8]{0:T(128)} %position_ref.1, f32[1,16]{1,0:T(1,128)} %bitcast.13, f32[1,16]{1,0:T(1,128)} %bitcast.14, f32[1,16]{1,0:T(1,128)} %bitcast.15, f32[3,16]{1,0:T(4,128)} %color_ref.1, s32[12,32,768]{2,1,0:T(8,128)} %bitcast.12, bf16[12,768,512]{2,1,0:T(8,128)(2,1)} %bitcast.10), custom_call_target="tpu_custom_call" | custom-call | tf_op jit(solution)/shard_map/pallas_call | solution.py:318
  98.2 2.1 %copy.10 = f32[4,1,96,512]{3,2,1,0:T(8,128)} copy(f32[4,1,96,512]{3,2,1,0:T(8,128)} %bitcast.11) | data formatting | bytes 1572864

commit v5 on v4

--- a/solution.py
+++ b/solution.py
@@ -166,15 +166,17 @@
     per_piece = piece // unit
     per_block = LANES // unit
 
-    def post(segment):
+    def post(segment, left):
+        cols = pl.ds(left, span)
+        slot = left // span
         there = lax.div(segment, per_piece)
         rows = pl.multiple_of(segment * unit, ROWS)
         inside = pl.multiple_of(lax.rem(segment, per_piece) * unit, ROWS)
         return pltpu.make_async_remote_copy(
-            src_ref=outbox.at[:, pl.ds(rows, unit), :],
-            dst_ref=inbox.at[me, :, pl.ds(inside, unit), :],
-            send_sem=send_sem.at[segment],
-            recv_sem=recv_sem.at[me, lax.rem(segment, per_piece)],
+            src_ref=outbox.at[:, pl.ds(rows, unit), cols],
+            dst_ref=inbox.at[me, :, pl.ds(inside, unit), cols],
+            send_sem=send_sem.at[segment, slot],
+            recv_sem=recv_sem.at[me, lax.rem(segment, per_piece), slot],
             device_id=(there, tile),
             device_id_type=MESH,
         )
@@ -187,15 +189,19 @@
         part = lax.rem(turn + me, blocks)
         area = lax.rem(side + away, 2)
         first = pl.multiple_of((area * blocks + part) * LANES, LANES)
-        entry_rows = [jnp.broadcast_to(tables[p : p + 1, :], (cells, LANES)) for p in range(6)]
-
-        def prepare(step, carry):
-            index = index_ref[step, :, pl.ds(first, LANES)]
-            for p in range(6):
-                found = jnp.take_along_axis(entry_rows[p], index, axis=1, mode="promise_in_bounds")
-                cell_params[step, p * cells : (p + 1) * cells, :] = found
-            for left in range(0, width, span):
-                cols = pl.ds(left, span)
+        cells_half = span // CELL
+        entry_rows = [jnp.broadcast_to(tables[p : p + 1, :], (cells_half, LANES)) for p in range(6)]
+
+        def march(left):
+            cols = pl.ds(left, span)
+            first_cell = left // CELL
+
+            def prepare(step, carry):
+                index = index_ref[step, first_cell : first_cell + cells_half, pl.ds(first, LANES)]
+                for p in range(6):
+                    found = jnp.take_along_axis(entry_rows[p], index, axis=1, mode="promise_in_bounds")
+                    begin = p * cells + first_cell
+                    cell_params[step, begin : begin + cells_half, :] = found
                 near = padded[step, pl.ds(pl.multiple_of(first + ROWS, ROWS), LANES), cols]
                 above = padded[step, pl.ds(first, ROWS), cols]
                 below = padded[step, pl.ds(pl.multiple_of(first + ROWS + LANES, ROWS), ROWS), cols]
@@ -205,66 +211,79 @@
                 grad_y[step, cols, :] = jnp.dot(
                     flipped.astype(jnp.bfloat16), step_y[...], preferred_element_type=jnp.float32
                 )
-            rim = slab[step, pl.ds(first, LANES), :]
-            edges = lax.dot_general(rim_pick[...], rim, transposed, preferred_element_type=jnp.float32)
-            turned[step, 0:RIM, :] = edges[:RIM]
-            turned[step, RIM + width : 2 * RIM + width, :] = edges[RIM:]
-            return carry
-
-        lax.fori_loop(0, depth_count, prepare, 0, unroll=2)
-
-        def column(cell, carry):
-            top = pl.multiple_of(cell * CELL, CELL)
-
-            def sample(step, carry):
-                red, green, blue, trans = carry
-                value = turned[step, pl.ds(top + RIM, CELL), :]
-                gx = turned[step, pl.ds(top + RIM + 1, CELL), :] - turned[step, pl.ds(top + RIM - 1, CELL), :]
-                gy = grad_y[step, pl.ds(top, CELL), :]
-
-                def param(number):
-                    row = cell_params[step, pl.ds(number * cells + cell, 1), :]
-                    return jnp.broadcast_to(row, (CELL, LANES))
-
-                energy = gx * gx + gy * gy
-                facing = shade_x * gx + shade_y * gy
-                base = 1.0 + energy
-                rough = pl.reciprocal(base, approx=True)
-                shade = 0.3 + facing * facing * (rough * (2.0 - base * rough))
-                scaled = param(0) * value - param(1)
-                keep = jnp.exp2(-(jnp.exp2(param(2) - scaled * scaled) * energy))
-                weight = trans * (1.0 - keep) * shade
-                return (
-                    red + weight * param(3),
-                    green + weight * param(4),
-                    blue + weight * param(5),
-                    trans * keep,
-                )
-
-            zero = jnp.zeros((CELL, LANES), jnp.float32)
-            start = (zero, zero, zero, zero + 1.0)
-            red, green, blue, trans = lax.fori_loop(0, depth_count, sample, start, unroll=True)
-            for channel, image in enumerate((red, green, blue, 1.0 - trans)):
-                image_turned[channel, pl.ds(top, CELL), :] = image
-            return carry
-
-        lax.fori_loop(0, cells, column, 0)
-
-        for channel in range(4):
-            for left in range(0, width, LANES):
-                flat = image_turned[channel, left : left + LANES, :].T
-                outbox[channel, pl.ds(first, LANES), left : left + LANES] = encode(flat)
-
-        def dispatch(number, carry):
-            segment = (area * blocks + part) * per_block + number
-
-            @pl.when(lax.div(segment, per_piece) != me)
-            def _():
-                post(segment).start()
-
-            return carry
-
-        lax.fori_loop(0, per_block, dispatch, 0)
+                if left == 0:
+                    rim = slab[step, pl.ds(first, LANES), :]
+                    edges = lax.dot_general(rim_pick[...], rim, transposed, preferred_element_type=jnp.float32)
+                    turned[step, 0:RIM, :] = edges[:RIM]
+                    turned[step, RIM + width : 2 * RIM + width, :] = edges[RIM:]
+                after = left + span
+                if after < width:
+                    beside = padded[
+                        step, pl.ds(pl.multiple_of(first + ROWS, ROWS), LANES), after : after + LANES
+                    ]
+                    ahead = lax.dot_general(
+                        half_eye[0:ROWS, 0:LANES], beside, transposed, preferred_element_type=jnp.float32
+                    )
+                    turned[step, RIM + after : 2 * RIM + after, :] = ahead[:RIM]
+                return carry
+
+            lax.fori_loop(0, depth_count, prepare, 0, unroll=4)
+
+            def column(cell, carry):
+                top = pl.multiple_of(cell * CELL, CELL)
+
+                def sample(step, carry):
+                    red, green, blue, trans = carry
+                    value = turned[step, pl.ds(top + RIM, CELL), :]
+                    gx = turned[step, pl.ds(top + RIM + 1, CELL), :] - turned[step, pl.ds(top + RIM - 1, CELL), :]
+                    gy = grad_y[step, pl.ds(top, CELL), :]
+
+                    def param(number):
+                        row = cell_params[step, pl.ds(number * cells + cell, 1), :]
+                        return jnp.broadcast_to(row, (CELL, LANES))
+
+                    energy = gx * gx + gy * gy
+                    facing = shade_x * gx + shade_y * gy
+                    base = 1.0 + energy
+                    rough = pl.reciprocal(base, approx=True)
+                    shade = 0.3 + facing * facing * (rough * (2.0 - base * rough))
+                    scaled = param(0) * value - param(1)
+                    keep = jnp.exp2(-(jnp.exp2(param(2) - scaled * scaled) * energy))
+                    weight = trans * (1.0 - keep) * shade
+                    return (
+                        red + weight * param(3),
+                        green + weight * param(4),
+                        blue + weight * param(5),
+                        trans * keep,
+                    )
+
+                zero = jnp.zeros((CELL, LANES), jnp.float32)
+                start = (zero, zero, zero, zero + 1.0)
+                red, green, blue, trans = lax.fori_loop(0, depth_count, sample, start, unroll=True)
+                for channel, image in enumerate((red, green, blue, 1.0 - trans)):
+                    image_turned[channel, pl.ds(top, CELL), :] = image
+                return carry
+
+            lax.fori_loop(first_cell, first_cell + cells_half, column, 0)
+
+            for channel in range(4):
+                for at in range(left, left + span, LANES):
+                    flat = image_turned[channel, at : at + LANES, :].T
+                    outbox[channel, pl.ds(first, LANES), at : at + LANES] = encode(flat)
+
+            def dispatch(number, carry):
+                segment = (area * blocks + part) * per_block + number
+
+                @pl.when(lax.div(segment, per_piece) != me)
+                def _():
+                    post(segment, left).start()
+
+                return carry
+
+            lax.fori_loop(0, per_block, dispatch, 0)
+
+        for left in range(0, width, span):
+            march(left)
         return carry
 
     lax.fori_loop(0, 2 * blocks, block, 0)
@@ -276,16 +295,17 @@
     def settle(number, carry):
         there = lax.rem(me + 1 + lax.div(number, per_piece), ranks)
         inside = lax.rem(number, per_piece)
-        post(there * per_piece + inside).wait_send()
         rows = pl.ds(pl.multiple_of(inside * unit, ROWS), unit)
-        pltpu.make_async_remote_copy(
-            src_ref=outbox.at[:, pl.ds(0, unit), :],
-            dst_ref=inbox.at[there, :, rows, :],
-            send_sem=send_sem.at[0],
-            recv_sem=recv_sem.at[there, inside],
-            device_id=(there, tile),
-            device_id_type=MESH,
-        ).wait_recv()
+        for left in range(0, width, span):
+            post(there * per_piece + inside, left).wait_send()
+            pltpu.make_async_remote_copy(
+                src_ref=outbox.at[:, pl.ds(0, unit), pl.ds(left, span)],
+                dst_ref=inbox.at[there, :, rows, pl.ds(left, span)],
+                send_sem=send_sem.at[0, 0],
+                recv_sem=recv_sem.at[there, inside, left // span],
+                device_id=(there, tile),
+                device_id_type=MESH,
+            ).wait_recv()
         return carry
 
     lax.fori_loop(0, (ranks - 1) * per_piece, settle, 0)
@@ -345,8 +365,8 @@
             pltpu.SemaphoreType.DMA,
             pltpu.SemaphoreType.DMA((2,)),
             pltpu.SemaphoreType.DMA((2,)),
-            pltpu.SemaphoreType.DMA((height // math.gcd(piece, LANES),)),
-            pltpu.SemaphoreType.DMA((ranks, piece // math.gcd(piece, LANES))),
+            pltpu.SemaphoreType.DMA((height // math.gcd(piece, LANES), width // (2 * LANES))),
+            pltpu.SemaphoreType.DMA((ranks, piece // math.gcd(piece, LANES), width // (2 * LANES))),
             pltpu.SemaphoreType.DMA,
         ],
         compiler_params=pltpu.CompilerParams(

time: 102 us -> 95.5 us (0.936); the launches traced: 100 us -> 95.3 us
  Pallas kernels: 98.2 us -> 93.3 us
    pallas_call x1, Pallas kernels: 98.2 us -> 93.3 us  [fused_device(): pl.pallas_call(functools.partial(march_kernel, ranks, tiles), out_shape=j...]
where the time goes in v5:
time: 95.5 us; the launch traced here: 95.3 us
  Pallas kernels  93.3 us (98%)
  local copies, waits for them, and re-layouts  2.06 us (2%)
    pallas_call x1, Pallas kernels, fused_device(): pl.pallas_call(functools.partial(march_kernel, ranks, tiles), out_shape=j...  93.3 us
    unnamed x1, local copies, waits for them, and re-layouts  2.06 us

profile of v5, /device:TPU:0, one launch (start us, length us, event | category | flops | bytes accessed | tf_op | source)
XLA Modules:
  0.0 95.3 jit_solution(13597676079791199791)
XLA Ops:
  0.0 93.3 %shard_map.73 = f32[4,96,512]{2,1,0:T(8,128)} custom-call(s32[8]{0:T(128)} %position_ref.1, f32[1,16]{1,0:T(1,128)} %bitcast.13, f32[1,16]{1,0:T(1,128)} %bitcast.14, f32[1,16]{1,0:T(1,128)} %bitcast.15, f32[3,16]{1,0:T(4,128)} %color_ref.1, s32[12,32,768]{2,1,0:T(8,128)} %bitcast.12, bf16[12,768,512]{2,1,0:T(8,128)(2,1)} %bitcast.10), custom_call_target="tpu_custom_call" | custom-call | tf_op jit(solution)/shard_map/pallas_call | solution.py:338
  93.3 2.1 %copy.10 = f32[4,1,96,512]{3,2,1,0:T(8,128)} copy(f32[4,1,96,512]{3,2,1,0:T(8,128)} %bitcast.11) | data formatting | bytes 1572864

commit v6 on v5

--- a/solution.py
+++ b/solution.py
@@ -47,11 +47,12 @@
     order,
     half_eye,
     rim_pick,
+    inner_pick,
     step_y,
     tables,
-    turned,
-    grad_y,
-    cell_params,
+    turned_parts,
+    grad_parts,
+    param_parts,
     image_turned,
     outbox,
     inbox,
@@ -129,6 +130,9 @@
     half_eye[...] = from_mask(eye_row == eye_col, 0.5)
     pick_row = lax.broadcasted_iota(jnp.int32, (ROWS, LANES), 0)
     pick_col = lax.broadcasted_iota(jnp.int32, (ROWS, LANES), 1)
+    wanted_left = jnp.logical_and(pick_row == RIM - 1, pick_col == LANES - 1)
+    wanted_right = jnp.logical_and(pick_row == RIM, pick_col == 0)
+    inner_pick[...] = from_mask(jnp.logical_or(wanted_left, wanted_right), 0.5)
     wanted_row = jnp.where(col_bit == 1, RIM - 1, RIM)
     wanted_col = jnp.where(col_bit == 1, LANES - 1, 0)
     rim_pick[...] = from_mask(jnp.logical_and(pick_row == wanted_row, pick_col == wanted_col), 0.5)
@@ -184,95 +188,110 @@
     blocks = height // LANES // 2
     transposed = (((1,), (1,)), ((), ()))
 
+    parts = width // span
+    cells_part = span // CELL
+    laps = math.gcd(depth_count, cells_part)
+
+    def spot(turn):
+        area = lax.rem(side + 1 - lax.div(turn, blocks), 2)
+        return area * blocks + lax.rem(turn + me, blocks)
+
+    def prepare(part, first, step):
+        left = part * span
+        cols = pl.ds(left, span)
+        turned = turned_parts[part]
+        middle = pl.ds(pl.multiple_of(first + ROWS, ROWS), LANES)
+        index = index_ref[step, part * cells_part : (part + 1) * cells_part, pl.ds(first, LANES)]
+        for p in range(6):
+            entries_wide = jnp.broadcast_to(tables[p : p + 1, :], (cells_part, LANES))
+            found = jnp.take_along_axis(entries_wide, index, axis=1, mode="promise_in_bounds")
+            param_parts[part][step, p * cells_part : (p + 1) * cells_part, :] = found
+        near = padded[step, middle, cols]
+        above = padded[step, pl.ds(first, ROWS), cols]
+        below = padded[step, pl.ds(pl.multiple_of(first + ROWS + LANES, ROWS), ROWS), cols]
+        rows = jnp.concatenate([near, above, below], axis=0)
+        flipped = lax.dot_general(half_eye[...], rows, transposed, preferred_element_type=jnp.float32)
+        turned[step, RIM : RIM + span, :] = flipped[:, :LANES]
+        grad_parts[part][step] = jnp.dot(
+            flipped.astype(jnp.bfloat16), step_y[...], preferred_element_type=jnp.float32
+        )
+
+        def edges(pick, beside):
+            return lax.dot_general(pick[...], beside, transposed, preferred_element_type=jnp.float32)
+
+        rim = slab[step, pl.ds(first, LANES), :]
+        before = edges(rim_pick, rim) if part == 0 else edges(inner_pick, padded[step, middle, left - LANES : left])
+        after = left + span
+        if part == parts - 1:
+            behind = edges(rim_pick, rim)
+        else:
+            behind = edges(inner_pick, padded[step, middle, after : after + LANES])
+        turned[step, 0:RIM, :] = before[:RIM]
+        turned[step, RIM + span : 2 * RIM + span, :] = behind[RIM:]
+
+    def march(part, cell):
+        turned = turned_parts[part]
+        grad_y = grad_parts[part]
+        params = param_parts[part]
+        top = pl.multiple_of(cell * CELL, CELL)
+
+        def sample(step, carry):
+            red, green, blue, trans = carry
+            value = turned[step, pl.ds(top + RIM, CELL), :]
+            gx = turned[step, pl.ds(top + RIM + 1, CELL), :] - turned[step, pl.ds(top + RIM - 1, CELL), :]
+            gy = grad_y[step, pl.ds(top, CELL), :]
+
+            def param(number):
+                row = params[step, pl.ds(number * cells_part + cell, 1), :]
+                return jnp.broadcast_to(row, (CELL, LANES))
+
+            energy = gx * gx + gy * gy
+            facing = shade_x * gx + shade_y * gy
+            base = 1.0 + energy
+            rough = pl.reciprocal(base, approx=True)
+            shade = 0.3 + facing * facing * (rough * (2.0 - base * rough))
+            scaled = param(0) * value - param(1)
+            keep = jnp.exp2(-(jnp.exp2(param(2) - scaled * scaled) * energy))
+            weight = trans * (1.0 - keep) * shade
+            return (
+                red + weight * param(3),
+                green + weight * param(4),
+                blue + weight * param(5),
+                trans * keep,
+            )
+
+        zero = jnp.zeros((CELL, LANES), jnp.float32)
+        start = (zero, zero, zero, zero + 1.0)
+        red, green, blue, trans = lax.fori_loop(0, depth_count, sample, start, unroll=True)
+        for channel, image in enumerate((red, green, blue, 1.0 - trans)):
+            image_turned[channel, pl.ds(top, CELL), :] = image
+
     def block(turn, carry):
-        away = 1 - lax.div(turn, blocks)
-        part = lax.rem(turn + me, blocks)
-        area = lax.rem(side + away, 2)
-        first = pl.multiple_of((area * blocks + part) * LANES, LANES)
-        cells_half = span // CELL
-        entry_rows = [jnp.broadcast_to(tables[p : p + 1, :], (cells_half, LANES)) for p in range(6)]
-
-        def march(left):
-            cols = pl.ds(left, span)
-            first_cell = left // CELL
-
-            def prepare(step, carry):
-                index = index_ref[step, first_cell : first_cell + cells_half, pl.ds(first, LANES)]
-                for p in range(6):
-                    found = jnp.take_along_axis(entry_rows[p], index, axis=1, mode="promise_in_bounds")
-                    begin = p * cells + first_cell
-                    cell_params[step, begin : begin + cells_half, :] = found
-                near = padded[step, pl.ds(pl.multiple_of(first + ROWS, ROWS), LANES), cols]
-                above = padded[step, pl.ds(first, ROWS), cols]
-                below = padded[step, pl.ds(pl.multiple_of(first + ROWS + LANES, ROWS), ROWS), cols]
-                rows = jnp.concatenate([near, above, below], axis=0)
-                flipped = lax.dot_general(half_eye[...], rows, transposed, preferred_element_type=jnp.float32)
-                turned[step, RIM + left : RIM + left + span, :] = flipped[:, :LANES]
-                grad_y[step, cols, :] = jnp.dot(
-                    flipped.astype(jnp.bfloat16), step_y[...], preferred_element_type=jnp.float32
-                )
-                if left == 0:
-                    rim = slab[step, pl.ds(first, LANES), :]
-                    edges = lax.dot_general(rim_pick[...], rim, transposed, preferred_element_type=jnp.float32)
-                    turned[step, 0:RIM, :] = edges[:RIM]
-                    turned[step, RIM + width : 2 * RIM + width, :] = edges[RIM:]
-                after = left + span
-                if after < width:
-                    beside = padded[
-                        step, pl.ds(pl.multiple_of(first + ROWS, ROWS), LANES), after : after + LANES
-                    ]
-                    ahead = lax.dot_general(
-                        half_eye[0:ROWS, 0:LANES], beside, transposed, preferred_element_type=jnp.float32
-                    )
-                    turned[step, RIM + after : 2 * RIM + after, :] = ahead[:RIM]
+        place = spot(turn)
+        first = pl.multiple_of(place * LANES, LANES)
+        later = pl.multiple_of(spot(lax.rem(turn + 1, 2 * blocks)) * LANES, LANES)
+
+        for part in range(parts):
+            following = (part + 1) % parts
+            upcoming = later if following == 0 else first
+
+            def lap(number, carry):
+                for extra in range(depth_count // laps):
+                    prepare(following, upcoming, number * (depth_count // laps) + extra)
+                for extra in range(cells_part // laps):
+                    march(part, number * (cells_part // laps) + extra)
                 return carry
 
-            lax.fori_loop(0, depth_count, prepare, 0, unroll=4)
-
-            def column(cell, carry):
-                top = pl.multiple_of(cell * CELL, CELL)
-
-                def sample(step, carry):
-                    red, green, blue, trans = carry
-                    value = turned[step, pl.ds(top + RIM, CELL), :]
-                    gx = turned[step, pl.ds(top + RIM + 1, CELL), :] - turned[step, pl.ds(top + RIM - 1, CELL), :]
-                    gy = grad_y[step, pl.ds(top, CELL), :]
-
-                    def param(number):
-                        row = cell_params[step, pl.ds(number * cells + cell, 1), :]
-                        return jnp.broadcast_to(row, (CELL, LANES))
-
-                    energy = gx * gx + gy * gy
-                    facing = shade_x * gx + shade_y * gy
-                    base = 1.0 + energy
-                    rough = pl.reciprocal(base, approx=True)
-                    shade = 0.3 + facing * facing * (rough * (2.0 - base * rough))
-                    scaled = param(0) * value - param(1)
-                    keep = jnp.exp2(-(jnp.exp2(param(2) - scaled * scaled) * energy))
-                    weight = trans * (1.0 - keep) * shade
-                    return (
-                        red + weight * param(3),
-                        green + weight * param(4),
-                        blue + weight * param(5),
-                        trans * keep,
-                    )
-
-                zero = jnp.zeros((CELL, LANES), jnp.float32)
-                start = (zero, zero, zero, zero + 1.0)
-                red, green, blue, trans = lax.fori_loop(0, depth_count, sample, start, unroll=True)
-                for channel, image in enumerate((red, green, blue, 1.0 - trans)):
-                    image_turned[channel, pl.ds(top, CELL), :] = image
-                return carry
-
-            lax.fori_loop(first_cell, first_cell + cells_half, column, 0)
-
+            lax.fori_loop(0, laps, lap, 0)
+
+            left = part * span
             for channel in range(4):
-                for at in range(left, left + span, LANES):
+                for at in range(0, span, LANES):
                     flat = image_turned[channel, at : at + LANES, :].T
-                    outbox[channel, pl.ds(first, LANES), at : at + LANES] = encode(flat)
+                    outbox[channel, pl.ds(first, LANES), left + at : left + at + LANES] = encode(flat)
 
             def dispatch(number, carry):
-                segment = (area * blocks + part) * per_block + number
+                segment = place * per_block + number
 
                 @pl.when(lax.div(segment, per_piece) != me)
                 def _():
@@ -281,11 +300,15 @@
                 return carry
 
             lax.fori_loop(0, per_block, dispatch, 0)
-
-        for left in range(0, width, span):
-            march(left)
         return carry
 
+    opening = pl.multiple_of(spot(0) * LANES, LANES)
+
+    def begin(step, carry):
+        prepare(0, opening, step)
+        return carry
+
+    lax.fori_loop(0, depth_count, begin, 0, unroll=4)
     lax.fori_loop(0, 2 * blocks, block, 0)
     mine = outbox.at[:, pl.ds(pl.multiple_of(me * piece, ROWS), piece), :]
     own = pltpu.make_async_copy(mine, inbox.at[me], own_sem)
@@ -335,6 +358,8 @@
     depth_count, height, width = samples.shape
     piece = height // ranks
     cells = index.shape[1]
+    span = 2 * LANES
+    parts = width // span
     image = pl.pallas_call(
         functools.partial(march_kernel, ranks, tiles),
         out_shape=jax.ShapeDtypeStruct((4, piece, width), jnp.float32),
@@ -354,12 +379,13 @@
             pltpu.SMEM((ranks,), jnp.int32),
             pltpu.VMEM((2 * LANES, 2 * LANES), jnp.bfloat16),
             pltpu.VMEM((ROWS, LANES), jnp.bfloat16),
+            pltpu.VMEM((ROWS, LANES), jnp.bfloat16),
             pltpu.VMEM((LANES + 2 * ROWS, LANES), jnp.bfloat16),
             pltpu.VMEM((8, LANES), jnp.float32),
-            pltpu.VMEM((depth_count, width + 2 * RIM, LANES), jnp.float32),
-            pltpu.VMEM((depth_count, width, LANES), jnp.float32),
-            pltpu.VMEM((depth_count, 6 * cells, LANES), jnp.float32),
-            pltpu.VMEM((4, width, LANES), jnp.float32),
+            [pltpu.VMEM((depth_count, span + 2 * RIM, LANES), jnp.float32)] * parts,
+            [pltpu.VMEM((depth_count, span, LANES), jnp.float32)] * parts,
+            [pltpu.VMEM((depth_count, 6 * (span // CELL), LANES), jnp.float32)] * parts,
+            pltpu.VMEM((4, span, LANES), jnp.float32),
             pltpu.VMEM((4, height, width), jnp.int16),
             pltpu.VMEM((ranks, 4, piece, width), jnp.int16),
             pltpu.SemaphoreType.DMA,
@@ -463,7 +489,7 @@
 def fits(ranks, tiles, shape):
     height, width = shape[2], shape[3]
     even = ranks % 2 == 0 and tiles == 4 and height % ranks == 0
-    return even and (height // ranks) % ROWS == 0 and width % (2 * LANES) == 0 and height % (2 * LANES) == 0
+    return even and (height // ranks) % ROWS == 0 and width % (2 * LANES) == 0 and width > 2 * LANES and height % (2 * LANES) == 0
 
 
 def solution(mesh):

time: 95.5 us -> 97.5 us (1.021)
  Pallas kernels: 93.3 us -> 95.2 us
    pallas_call x1, Pallas kernels: 93.3 us -> 95.2 us  [fused_device(): pl.pallas_call(functools.partial(march_kernel, ranks, tiles), out_shape=j...]
where the time goes in v6:
time: 97.5 us; the launch traced here: 97.3 us
  Pallas kernels  95.2 us (98%)
  local copies, waits for them, and re-layouts  2.06 us (2%)
    pallas_call x1, Pallas kernels, fused_device(): pl.pallas_call(functools.partial(march_kernel, ranks, tiles), out_shape=j...  95.2 us
    unnamed x1, local copies, waits for them, and re-layouts  2.06 us

profile of v6, /device:TPU:0, one launch (start us, length us, event | category | flops | bytes accessed | tf_op | source)
XLA Modules:
  0.0 97.3 jit_solution(15660088910057889950)
XLA Ops:
  0.0 95.2 %shard_map.73 = f32[4,96,512]{2,1,0:T(8,128)} custom-call(s32[8]{0:T(128)} %position_ref.1, f32[1,16]{1,0:T(1,128)} %bitcast.13, f32[1,16]{1,0:T(1,128)} %bitcast.14, f32[1,16]{1,0:T(1,128)} %bitcast.15, f32[3,16]{1,0:T(4,128)} %color_ref.1, s32[12,32,768]{2,1,0:T(8,128)} %bitcast.12, bf16[12,768,512]{2,1,0:T(8,128)(2,1)} %bitcast.10), custom_call_target="tpu_custom_call" | custom-call | tf_op jit(solution)/shard_map/pallas_call | solution.py:363
  95.2 2.1 %copy.10 = f32[4,1,96,512]{3,2,1,0:T(8,128)} copy(f32[4,1,96,512]{3,2,1,0:T(8,128)} %bitcast.11) | data formatting | bytes 1572864

commit v7 on v5

--- a/solution.py
+++ b/solution.py
@@ -27,7 +27,7 @@
 
 def decode(code):
     steps = code.astype(jnp.int32).astype(jnp.float32)
-    value = jnp.exp2((steps + float(MID_CODE)) * (-1.0 / SCALE))
+    value = jnp.exp((steps + float(MID_CODE)) * (-1.0 / (SCALE * LOG2E)))
     return jnp.where(steps >= TOP_CODE - MID_CODE, 0.0, value)
 
 
@@ -139,8 +139,8 @@
     step_y[...] = plus - from_mask(window_at == lane_at - 1, 1.0)
 
     entries = center_ref.shape[1]
-    gain = math.sqrt(0.5 * LOG2E) / width_ref[...]
-    level = jnp.log(peak_ref[...] * (LOG2E / (depth_count * ranks))) * LOG2E
+    gain = math.sqrt(0.5) / width_ref[...]
+    level = jnp.log(peak_ref[...] * (1.0 / (depth_count * ranks)))
     tables[...] = jnp.zeros(tables.shape, jnp.float32)
     tables[0:1, 0:entries] = gain + gain
     tables[1:2, 0:entries] = gain * center_ref[...]
@@ -248,7 +248,7 @@
                     rough = pl.reciprocal(base, approx=True)
                     shade = 0.3 + facing * facing * (rough * (2.0 - base * rough))
                     scaled = param(0) * value - param(1)
-                    keep = jnp.exp2(-(jnp.exp2(param(2) - scaled * scaled) * energy))
+                    keep = jnp.exp(-(jnp.exp(param(2) - scaled * scaled) * energy))
                     weight = trans * (1.0 - keep) * shade
                     return (
                         red + weight * param(3),
@@ -321,7 +321,7 @@
                 return tuple(images[c] + clear * decode(inbox[rank, c, rows, cols]) for c in range(4))
 
             zero = jnp.zeros((ROWS, span), jnp.float32)
-            images = lax.fori_loop(0, ranks, layer, (zero,) * 4, unroll=2)
+            images = lax.fori_loop(0, ranks, layer, (zero,) * 4, unroll=True)
             for c in range(4):
                 out_ref[c, rows, cols] = images[c]
         return carry

time: 95.5 us -> 94.6 us (level)
  Pallas kernels: 93.3 us -> 92.3 us
    pallas_call x1, Pallas kernels: 93.3 us -> 92.3 us  [fused_device(): pl.pallas_call(functools.partial(march_kernel, ranks, tiles), out_shape=j...]
where the time goes in v7:
time: 94.6 us; the launch traced here: 94.4 us
  Pallas kernels  92.3 us (98%)
  local copies, waits for them, and re-layouts  2.06 us (2%)
    pallas_call x1, Pallas kernels, fused_device(): pl.pallas_call(functools.partial(march_kernel, ranks, tiles), out_shape=j...  92.3 us
    unnamed x1, local copies, waits for them, and re-layouts  2.06 us

profile of v7, /device:TPU:0, one launch (start us, length us, event | category | flops | bytes accessed | tf_op | source)
XLA Modules:
  0.0 94.4 jit_solution(8134994680805967598)
XLA Ops:
  0.0 92.3 %shard_map.73 = f32[4,96,512]{2,1,0:T(8,128)} custom-call(s32[8]{0:T(128)} %position_ref.1, f32[1,16]{1,0:T(1,128)} %bitcast.13, f32[1,16]{1,0:T(1,128)} %bitcast.14, f32[1,16]{1,0:T(1,128)} %bitcast.15, f32[3,16]{1,0:T(4,128)} %color_ref.1, s32[12,32,768]{2,1,0:T(8,128)} %bitcast.12, bf16[12,768,512]{2,1,0:T(8,128)(2,1)} %bitcast.10), custom_call_target="tpu_custom_call" | custom-call | tf_op jit(solution)/shard_map/pallas_call | solution.py:338
  92.3 2.1 %copy.10 = f32[4,1,96,512]{3,2,1,0:T(8,128)} copy(f32[4,1,96,512]{3,2,1,0:T(8,128)} %bitcast.11) | data formatting | bytes 1572864
